TPU v7x, 32 devices: a whole 2x2x4 slice. The times are simulated.
32 devices in a mesh: strip: 8 (over z, x), sub: 4 (over y, core).
Axes of the slice: x: 2, y: 2, z: 4, core: 2. Of those that a mesh axis runs over, the one named last changes fastest.
Arguments:
- features: bfloat16 [32768, 128], P(('strip', 'sub')), may hold values from -6 to 6
- position: bfloat16 [2, 32768, 128], P(None, ('strip', 'sub')), may hold values from -6 to 6
- cotangent: bfloat16 [32768, 128], P(('strip', 'sub')), may hold values from -6 to 6
- w_qkv: bfloat16 [2, 128, 384], replicated, may hold values from -0.5 to 0.5
- w_out: bfloat16 [2, 128, 128], replicated, may hold values from -1.5 to 1.5
- w_up: bfloat16 [2, 128, 256], replicated, may hold values from -0.5 to 0.5
- w_down: bfloat16 [2, 256, 128], replicated, may hold values from -0.375 to 0.375
- b_up: float32 [2, 256], replicated, may hold values from -3 to 3
- gains: float32 [2, 2, 128], replicated, may hold values from 0.5 to 1.5
- shifts: float32 [2, 4, 128], replicated, may hold values from -3 to 3
- window: int32 [32768], P(('strip', 'sub')), may hold values from 0 to 31
- shifted_window: int32 [32768], P(('strip', 'sub')), may hold values from 0 to 63
- dest: int32 [32768], P(('strip', 'sub')), may hold values from 0 to 7, as said below
- slot: int32 [32768], P(('strip', 'sub')), may hold values from 0 to 255, as said below
- valid: int32 [32768], P(('strip', 'sub')), may hold values 0 or 1
Outputs:
- output: bfloat16 [32768, 128], P(('strip', 'sub'))
- grad_features: float32 [32768, 128], P(('strip', 'sub'))
- grad_w_qkv: float32 [2, 128, 384], replicated
- grad_w_out: float32 [2, 128, 128], replicated
- grad_w_up: float32 [2, 128, 256], replicated
- grad_w_down: float32 [2, 256, 128], replicated
- grad_b_up: float32 [2, 256], replicated
- grad_gains: float32 [2, 2, 128], replicated
- grad_shifts: float32 [2, 4, 128], replicated
Inputs may be any that keep to these rules, and one draw needn't show every extreme that they name: On each device no two pillars share both dest and slot; the pillars of one device with one dest have slots 0 up to their count minus one. In every draw one strip receives 256 pillars from every device and another receives none. Some pillar of every device has slot 255.
All inputs are finite; a program needn't handle non-finite values. No bound on the sum of `valid` on one device may be relied on, other than what follows from the above.
Results may differ from a plain program's by a relative error of at most 0.019.
The roundings to bfloat16 on the way count: a program that leaves them out, or rounds other values in their place, can miss the bound.
Values may be sent and summed in bfloat16 or wider, within the bound.
No kernel may reach another device: no remote copies, remote signals or barrier semaphores. Data moves between devices by JAX's collectives and lax.ppermute only.
A program may use at most 192 MiB of HBM per device.

v0:
```python
import jax
import jax.numpy as jnp
from jax import lax
from jax.sharding import PartitionSpec as P

HEADS = 8


EPS = 1e-05
NEGATIVE = -1e30


def outer_sum(left, right):
    return lax.dot_general(
        left, right, (((0,), (0,)), ((), ())), preferred_element_type=jnp.float32
    )


def times_transposed(left, right):
    return lax.dot_general(
        left, right, (((1,), (1,)), ((), ())), preferred_element_type=jnp.float32
    )


def norm_forward(hidden, gain, shift):
    average = jnp.mean(hidden, axis=-1, keepdims=True)
    centered = hidden - average
    inverse = lax.rsqrt(jnp.mean(centered * centered, axis=-1, keepdims=True) + EPS)
    normed = centered * inverse
    return (normed * gain + shift, normed, inverse)


def norm_backward(upstream, normed, inverse, gain):
    scaled = upstream * gain
    center_term = jnp.mean(scaled, axis=-1, keepdims=True)
    normal_term = normed * jnp.mean(scaled * normed, axis=-1, keepdims=True)
    return (
        inverse * (scaled - center_term - normal_term),
        jnp.sum(upstream * normed, axis=0),
        jnp.sum(upstream, axis=0),
    )


def block_scores(query_blk, query_ids, head_keys, key_ids, key_live, scale):
    scores = (
        jnp.einsum("ihd,jhd->hij", query_blk, head_keys, preferred_element_type=jnp.float32) * scale
    )
    allowed = (query_ids[:, None] == key_ids[None, :]) & (key_live[None, :] > 0)
    return jnp.where(allowed[None], scores, NEGATIVE)


def attend_forward(queries, keys, values, ids, live, scale):
    row_total, row_width = queries.shape
    head_size = row_width // HEADS
    block_rows = min(512, row_total)
    block_count = row_total // block_rows
    head_keys = keys.reshape(row_total, HEADS, head_size)
    head_values = values.reshape(row_total, HEADS, head_size)

    def one_block(items):
        query_blk, query_ids = items
        masked = block_scores(query_blk, query_ids, head_keys, ids, live, scale)
        highest = jnp.max(masked, axis=-1, keepdims=True)
        exponent = jnp.exp(masked - highest)
        summed = jnp.sum(exponent, axis=-1, keepdims=True)
        attention = (exponent / summed).astype(jnp.bfloat16)
        mixed = jnp.einsum(
            "hij,jhd->ihd", attention, head_values, preferred_element_type=jnp.float32
        )
        return (mixed.reshape(block_rows, row_width), highest[..., 0] + jnp.log(summed[..., 0]))

    mixed, log_total = lax.map(
        one_block,
        (
            queries.reshape(block_count, block_rows, HEADS, head_size),
            ids.reshape(block_count, block_rows),
        ),
    )
    return (mixed.reshape(row_total, row_width), log_total)


def attend_backward(queries, keys, values, ids, live, log_total, upstream, scale):
    row_total, row_width = queries.shape
    head_size = row_width // HEADS
    block_rows = min(512, row_total)
    block_count = row_total // block_rows
    head_keys = keys.reshape(row_total, HEADS, head_size)
    head_values = values.reshape(row_total, HEADS, head_size)
    zeros = jnp.zeros((row_total, HEADS, head_size), jnp.float32)

    def one_block(carry, items):
        key_grad, value_grad = carry
        query_blk, query_ids, block_log, grad_blk = items
        masked = block_scores(query_blk, query_ids, head_keys, ids, live, scale)
        attention = jnp.exp(masked - block_log[..., None])
        prob_grad = jnp.einsum(
            "ihd,jhd->hij", grad_blk, head_values, preferred_element_type=jnp.float32
        )
        value_grad = value_grad + jnp.einsum(
            "hij,ihd->jhd",
            attention.astype(jnp.bfloat16),
            grad_blk,
            preferred_element_type=jnp.float32,
        )
        score_grad = attention * (
            prob_grad - jnp.sum(attention * prob_grad, axis=-1, keepdims=True)
        )
        score_grad = score_grad.astype(jnp.bfloat16)
        query_grad = (
            jnp.einsum("hij,jhd->ihd", score_grad, head_keys, preferred_element_type=jnp.float32)
            * scale
        )
        key_grad = (
            key_grad
            + jnp.einsum("hij,ihd->jhd", score_grad, query_blk, preferred_element_type=jnp.float32)
            * scale
        )
        return ((key_grad, value_grad), query_grad.reshape(block_rows, row_width))

    items = (
        queries.reshape(block_count, block_rows, HEADS, head_size),
        ids.reshape(block_count, block_rows),
        log_total,
        upstream.reshape(block_count, block_rows, HEADS, head_size),
    )
    (key_grad, value_grad), query_grad = lax.scan(one_block, (zeros, zeros), items)
    return (
        query_grad.reshape(row_total, row_width),
        key_grad.reshape(row_total, row_width),
        value_grad.reshape(row_total, row_width),
    )


def layer_forward(inputs, placing, ids, live, weights, level):
    w_qkv, w_out, w_up, w_down, b_up, gains, shifts = weights
    row_width = inputs.shape[1]
    scale = (row_width // HEADS) ** (-0.5)
    joined = (inputs.astype(jnp.float32) + placing.astype(jnp.float32)).astype(jnp.bfloat16)
    query_key = jnp.dot(
        joined, w_qkv[level, :, : 2 * row_width], preferred_element_type=jnp.float32
    ).astype(jnp.bfloat16)
    values = jnp.dot(
        inputs, w_qkv[level, :, 2 * row_width :], preferred_element_type=jnp.float32
    ).astype(jnp.bfloat16)
    mixed, log_total = attend_forward(
        query_key[:, :row_width], query_key[:, row_width:], values, ids, live, scale
    )
    mixed_low = mixed.astype(jnp.bfloat16)
    attended = (
        jnp.dot(mixed_low, w_out[level], preferred_element_type=jnp.float32) + shifts[level, 0]
    )
    first_out, normed_one, inverse_one = norm_forward(
        inputs.astype(jnp.float32) + attended, gains[level, 0], shifts[level, 1]
    )
    first_low = first_out.astype(jnp.bfloat16)
    before = jnp.dot(first_low, w_up[level], preferred_element_type=jnp.float32) + b_up[level]
    activated = jax.nn.gelu(before).astype(jnp.bfloat16)
    branch = (
        jnp.dot(activated, w_down[level], preferred_element_type=jnp.float32) + shifts[level, 2]
    )
    result, normed_two, inverse_two = norm_forward(
        first_out + branch, gains[level, 1], shifts[level, 3]
    )
    stored = (
        joined,
        query_key,
        values,
        log_total,
        mixed_low,
        normed_one,
        inverse_one,
        first_low,
        before,
        activated,
        normed_two,
        inverse_two,
    )
    return (result * live.astype(jnp.float32)[:, None], stored)


def layer_backward(upstream, inputs, ids, live, weights, level, stored):
    w_qkv, w_out, w_up, w_down, b_up, gains, shifts = weights
    (
        joined,
        query_key,
        values,
        log_total,
        mixed_low,
        normed_one,
        inverse_one,
        first_low,
        before,
        activated,
        normed_two,
        inverse_two,
    ) = stored
    row_width = inputs.shape[1]
    scale = (row_width // HEADS) ** (-0.5)
    upstream = upstream * live.astype(jnp.float32)[:, None]
    second_grad, gain_two, bias_two = norm_backward(
        upstream, normed_two, inverse_two, gains[level, 1]
    )
    branch_low = second_grad.astype(jnp.bfloat16)
    down_grad = outer_sum(activated, branch_low)
    down_bias = jnp.sum(branch_low.astype(jnp.float32), axis=0)
    _, gelu_pull = jax.vjp(jax.nn.gelu, before)
    before_low = gelu_pull(times_transposed(branch_low, w_down[level]))[0].astype(jnp.bfloat16)
    up_grad = outer_sum(first_low, before_low)
    up_bias = jnp.sum(before_low.astype(jnp.float32), axis=0)
    first_grad = second_grad + times_transposed(before_low, w_up[level])
    residual_grad, gain_one, bias_one = norm_backward(
        first_grad, normed_one, inverse_one, gains[level, 0]
    )
    attended_low = residual_grad.astype(jnp.bfloat16)
    out_grad = outer_sum(mixed_low, attended_low)
    out_bias = jnp.sum(attended_low.astype(jnp.float32), axis=0)
    mixed_grad = times_transposed(attended_low, w_out[level]).astype(jnp.bfloat16)
    query_grad, key_grad, value_grad = attend_backward(
        query_key[:, :row_width],
        query_key[:, row_width:],
        values,
        ids,
        live,
        log_total,
        mixed_grad,
        scale,
    )
    pair_low = jnp.concatenate([query_grad, key_grad], axis=1).astype(jnp.bfloat16)
    value_low = value_grad.astype(jnp.bfloat16)
    qkv_grad = jnp.concatenate([outer_sum(joined, pair_low), outer_sum(inputs, value_low)], axis=1)
    input_grad = (
        residual_grad
        + times_transposed(pair_low, w_qkv[level, :, : 2 * row_width])
        + times_transposed(value_low, w_qkv[level, :, 2 * row_width :])
    )
    gain_grads = jnp.stack([gain_one, gain_two])
    shift_grads = jnp.stack([out_bias, bias_one, down_bias, bias_two])
    return (input_grad, (qkv_grad, out_grad, up_grad, down_grad, up_bias, gain_grads, shift_grads))


def local(
    features,
    position,
    cotangent,
    w_qkv,
    w_out,
    w_up,
    w_down,
    b_up,
    gains,
    shifts,
    window,
    shifted_window,
    dest,
    slot,
    valid,
):
    strip_count = lax.axis_size("strip")
    row_total, row_width = features.shape
    capacity = 2 * row_total // strip_count
    buffer_rows = strip_count * capacity
    place = dest * capacity + slot
    weights = (w_qkv, w_out, w_up, w_down, b_up, gains, shifts)

    def spread(source):
        return jnp.zeros((buffer_rows, source.shape[1]), source.dtype).at[place].set(source)

    out_zero, stored_zero = layer_forward(features, position[0], window, valid, weights, 0)
    out_zero_low = out_zero.astype(jnp.bfloat16)
    meta_buffer = spread(jnp.stack([shifted_window, valid], axis=1))
    arrived, meta_in = (
        lax.all_to_all(
            spread(jnp.concatenate([out_zero_low, position[1]], axis=1)),
            "strip",
            split_axis=0,
            concat_axis=0,
            tiled=True,
        ),
        lax.all_to_all(meta_buffer, "strip", split_axis=0, concat_axis=0, tiled=True),
    )
    cot_in = lax.all_to_all(spread(cotangent), "strip", split_axis=0, concat_axis=0, tiled=True)
    inputs_two = arrived[:, :row_width]
    placing_two = arrived[:, row_width : 2 * row_width]
    ids_two = meta_in[:, 0]
    live_two = meta_in[:, 1]
    out_one, stored_one = layer_forward(inputs_two, placing_two, ids_two, live_two, weights, 1)
    out_one_low = out_one.astype(jnp.bfloat16)
    grad_two, grads_one = layer_backward(
        cot_in.astype(jnp.float32), inputs_two, ids_two, live_two, weights, 1, stored_one
    )
    grad_two_low = grad_two.astype(jnp.bfloat16)
    output_rows = lax.all_to_all(out_one_low, "strip", split_axis=0, concat_axis=0, tiled=True)
    grad_rows = lax.all_to_all(grad_two_low, "strip", split_axis=0, concat_axis=0, tiled=True)
    output = output_rows[place]
    grad_zero_in = grad_rows[place].astype(jnp.float32)
    grad_features, grads_zero = layer_backward(
        grad_zero_in, features, window, valid, weights, 0, stored_zero
    )
    stacked = tuple((jnp.stack([early, later]) for early, later in zip(grads_zero, grads_one)))
    totals = lax.psum(stacked, ("strip", "sub"))
    return (
        output,
        grad_features,
        totals[0],
        totals[1],
        totals[2],
        totals[3],
        totals[4],
        totals[5],
        totals[6],
    )


def solution(mesh):
    placed = (
        P(("strip", "sub"), None),
        P(None, ("strip", "sub"), None),
        P(("strip", "sub"), None),
        P(),
        P(),
        P(),
        P(),
        P(),
        P(),
        P(),
        P(("strip", "sub")),
        P(("strip", "sub")),
        P(("strip", "sub")),
        P(("strip", "sub")),
        P(("strip", "sub")),
    )
    return jax.shard_map(
        local,
        mesh=mesh,
        in_specs=placed,
        out_specs=(
            P(("strip", "sub"), None),
            P(("strip", "sub"), None),
            P(),
            P(),
            P(),
            P(),
            P(),
            P(),
            P(),
        ),
        check_vma=False,
    )
```

profile of v0, /device:TPU:0, one launch (start us, length us, event | category | flops | bytes accessed | tf_op | source)
XLA Modules:
  0.0 1008.4 jit_solution(9622895269207576433)
XLA Ops:
  13.7 7.3 all-to-all-start.1
  29.0 27.8 %while.54 = (s32[]{:T(128)}, bf16[2,512,128]{2,1,0:T(8,128)(2,1)S(1)}, f32[2,8,512]{2,1,0:T(8,128)S(1)}, s32[2,512]{1,0:T(2,128)S(1)}, s32[1024]{0:T(1024)}, /*i...) while((s32[]{:T(128)}, ...), condition=%wide.region_3.4_spmd, body=%wide.region_0.3_spmd.sunk | while | flops 319812608 | bytes 53887100 | solution.py:72
  64.7 6.2 all-to-all-start.3
  78.0 6.9 all-to-all-done.3
  92.8 21.3 %all-to-all-done = bf16[8,256,256]{2,1,0:T(8,128)(2,1)S(1)} async-done(((bf16[8,256,256]{2,1,0:T(8,128)(2,1)}), bf16[8,256,256]{2,1,0:T(8,128)(2,1)S(1)}, u32[]{:S(2)}, u32[]{:S(2)}) %all-to-all-start) | async-done | bytes 1048608 | tf_op jit(solution)/shard_map/all_to_all | solution.py:272
  120.3 181.5 %while.55 = (s32[]{:T(128)}, bf16[4,512,128]{2,1,0:T(8,128)(2,1)}, f32[4,8,512]{2,1,0:T(8,128)}, s32[4,512]{1,0:T(4,128)}, s32[2048,1]{0,1:T(1,128)S(1)}, /*inde...) while((s32[]{:T(128)}, bf16[4,512,128]{2,1,0:T(8,128)(2,1)}, ...), condition=%wide.region_13.14_spmd, body=%wide.region_10.13_spmd.sunk | while | flops 639629312 | bytes 106850424 | solution.py:72
  121.9 13.6 %fusion.242 = (f32[8,512]{1,0:T(8,128)S(1)}, f32[8,512,2048]{2,1,0:T(8,128)}) fusion(pred[512,2048]{1,0:T(8,128)(4,1)S(1)} %compare_and_fusion.9, bf16[2048,8,16]{0,2,1:T(8,128)(2,1)S(1)} %get-tuple-element.1022, bf16[4,512,8,16]{1,3,2,0:T(8,128)(2,1)S(1)} %get-tuple-element.1021, s32[]{:T(128)S(6)} %copy.192), kind=kOutput, calls=%fused_computation.54.clone.1 | convolution fusion | flops 293597184 | bytes 35274756 | tf_op jit(solution)/shard_map/while/body/eval_jaxpr/ihd,jhd->hij/dot_general | solution.py:46
  135.5 15.0 %fusion.243 = f32[8,512]{1,0:T(8,128)S(1)} fusion(f32[8,512,2048]{2,1,0:T(8,128)} %get-tuple-element.935, f32[8,512]{1,0:T(8,128)S(1)} %get-tuple-element.936, pred[512,2048]{1,0:T(8,128)(4,1)S(1)} %compare_and_fusion.9), kind=kLoop, calls=%fused_computation.55.clone.1 | loop fusion | flops 33550336 | bytes 34635776 | tf_op jit(solution)/shard_map/while/body/eval_jaxpr/reduce_sum | solution.py:65
  150.5 13.8 %fusion.244 = bf16[8,512,16]{1,2,0:T(8,128)(2,1)S(1)} fusion(bf16[2048,8,16]{0,2,1:T(8,128)(2,1)S(1)} %get-tuple-element.1023, f32[8,512,2048]{2,1,0:T(8,128)} %get-tuple-element.935, f32[8,512]{1,0:T(8,128)S(1)} %fusion.243, f32[8,512]{1,0:T(8,128)S(1)} %get-tuple-element.936, pred[512,2048]{1,0:T(8,128)(4,1)S(1)} %compare_and_fusion.9), kind=kOutput, calls=%fused_computation.56.clone.1 | convolution fusion | flops 310378496 | bytes 35291136 | tf_op jit(solution)/shard_map/while/body/eval_jaxpr/hij,jhd->ihd/dot_general | solution.py:67
  167.1 13.6 %fusion.242 = (f32[8,512]{1,0:T(8,128)S(1)}, f32[8,512,2048]{2,1,0:T(8,128)}) fusion(pred[512,2048]{1,0:T(8,128)(4,1)S(1)} %compare_and_fusion.9, bf16[2048,8,16]{0,2,1:T(8,128)(2,1)S(1)} %get-tuple-element.1022, bf16[4,512,8,16]{1,3,2,0:T(8,128)(2,1)S(1)} %get-tuple-element.1021, s32[]{:T(128)S(6)} %copy.192), kind=kOutput, calls=%fused_computation.54.clone.1 | convolution fusion | flops 293597184 | bytes 35274756 | tf_op jit(solution)/shard_map/while/body/eval_jaxpr/ihd,jhd->hij/dot_general | solution.py:46
  180.7 15.0 %fusion.243 = f32[8,512]{1,0:T(8,128)S(1)} fusion(f32[8,512,2048]{2,1,0:T(8,128)} %get-tuple-element.935, f32[8,512]{1,0:T(8,128)S(1)} %get-tuple-element.936, pred[512,2048]{1,0:T(8,128)(4,1)S(1)} %compare_and_fusion.9), kind=kLoop, calls=%fused_computation.55.clone.1 | loop fusion | flops 33550336 | bytes 34635776 | tf_op jit(solution)/shard_map/while/body/eval_jaxpr/reduce_sum | solution.py:65
  195.7 13.8 %fusion.244 = bf16[8,512,16]{1,2,0:T(8,128)(2,1)S(1)} fusion(bf16[2048,8,16]{0,2,1:T(8,128)(2,1)S(1)} %get-tuple-element.1023, f32[8,512,2048]{2,1,0:T(8,128)} %get-tuple-element.935, f32[8,512]{1,0:T(8,128)S(1)} %fusion.243, f32[8,512]{1,0:T(8,128)S(1)} %get-tuple-element.936, pred[512,2048]{1,0:T(8,128)(4,1)S(1)} %compare_and_fusion.9), kind=kOutput, calls=%fused_computation.56.clone.1 | convolution fusion | flops 310378496 | bytes 35291136 | tf_op jit(solution)/shard_map/while/body/eval_jaxpr/hij,jhd->ihd/dot_general | solution.py:67
  212.4 13.6 %fusion.242 = (f32[8,512]{1,0:T(8,128)S(1)}, f32[8,512,2048]{2,1,0:T(8,128)}) fusion(pred[512,2048]{1,0:T(8,128)(4,1)S(1)} %compare_and_fusion.9, bf16[2048,8,16]{0,2,1:T(8,128)(2,1)S(1)} %get-tuple-element.1022, bf16[4,512,8,16]{1,3,2,0:T(8,128)(2,1)S(1)} %get-tuple-element.1021, s32[]{:T(128)S(6)} %copy.192), kind=kOutput, calls=%fused_computation.54.clone.1 | convolution fusion | flops 293597184 | bytes 35274756 | tf_op jit(solution)/shard_map/while/body/eval_jaxpr/ihd,jhd->hij/dot_general | solution.py:46
  225.9 15.0 %fusion.243 = f32[8,512]{1,0:T(8,128)S(1)} fusion(f32[8,512,2048]{2,1,0:T(8,128)} %get-tuple-element.935, f32[8,512]{1,0:T(8,128)S(1)} %get-tuple-element.936, pred[512,2048]{1,0:T(8,128)(4,1)S(1)} %compare_and_fusion.9), kind=kLoop, calls=%fused_computation.55.clone.1 | loop fusion | flops 33550336 | bytes 34635776 | tf_op jit(solution)/shard_map/while/body/eval_jaxpr/reduce_sum | solution.py:65
  240.9 13.8 %fusion.244 = bf16[8,512,16]{1,2,0:T(8,128)(2,1)S(1)} fusion(bf16[2048,8,16]{0,2,1:T(8,128)(2,1)S(1)} %get-tuple-element.1023, f32[8,512,2048]{2,1,0:T(8,128)} %get-tuple-element.935, f32[8,512]{1,0:T(8,128)S(1)} %fusion.243, f32[8,512]{1,0:T(8,128)S(1)} %get-tuple-element.936, pred[512,2048]{1,0:T(8,128)(4,1)S(1)} %compare_and_fusion.9), kind=kOutput, calls=%fused_computation.56.clone.1 | convolution fusion | flops 310378496 | bytes 35291136 | tf_op jit(solution)/shard_map/while/body/eval_jaxpr/hij,jhd->ihd/dot_general | solution.py:67
  257.6 13.6 %fusion.242 = (f32[8,512]{1,0:T(8,128)S(1)}, f32[8,512,2048]{2,1,0:T(8,128)}) fusion(pred[512,2048]{1,0:T(8,128)(4,1)S(1)} %compare_and_fusion.9, bf16[2048,8,16]{0,2,1:T(8,128)(2,1)S(1)} %get-tuple-element.1022, bf16[4,512,8,16]{1,3,2,0:T(8,128)(2,1)S(1)} %get-tuple-element.1021, s32[]{:T(128)S(6)} %copy.192), kind=kOutput, calls=%fused_computation.54.clone.1 | convolution fusion | flops 293597184 | bytes 35274756 | tf_op jit(solution)/shard_map/while/body/eval_jaxpr/ihd,jhd->hij/dot_general | solution.py:46
  271.2 15.0 %fusion.243 = f32[8,512]{1,0:T(8,128)S(1)} fusion(f32[8,512,2048]{2,1,0:T(8,128)} %get-tuple-element.935, f32[8,512]{1,0:T(8,128)S(1)} %get-tuple-element.936, pred[512,2048]{1,0:T(8,128)(4,1)S(1)} %compare_and_fusion.9), kind=kLoop, calls=%fused_computation.55.clone.1 | loop fusion | flops 33550336 | bytes 34635776 | tf_op jit(solution)/shard_map/while/body/eval_jaxpr/reduce_sum | solution.py:65
  286.2 13.8 %fusion.244 = bf16[8,512,16]{1,2,0:T(8,128)(2,1)S(1)} fusion(bf16[2048,8,16]{0,2,1:T(8,128)(2,1)S(1)} %get-tuple-element.1023, f32[8,512,2048]{2,1,0:T(8,128)} %get-tuple-element.935, f32[8,512]{1,0:T(8,128)S(1)} %fusion.243, f32[8,512]{1,0:T(8,128)S(1)} %get-tuple-element.936, pred[512,2048]{1,0:T(8,128)(4,1)S(1)} %compare_and_fusion.9), kind=kOutput, calls=%fused_computation.56.clone.1 | convolution fusion | flops 310378496 | bytes 35291136 | tf_op jit(solution)/shard_map/while/body/eval_jaxpr/hij,jhd->ihd/dot_general | solution.py:67
  327.1 381.3 %while.56 = (s32[]{:T(128)}, f32[2048,8,16]{0,2,1:T(8,128)S(1)}, f32[2048,8,16]{0,2,1:T(8,128)}, bf16[4,512,128]{2,1,0:T(8,128)(2,1)}, bf16[4,512,8,16]{1,3,2,0:...) while((s32[]{:T(128)}, f32[2048,8,16]{0,2,1:T(8,128)S(1)}, ...), condition=%wide.region_25.26_spmd.clone, body=%wide.region_23.25_spmd.clone.sunk | while | flops 1421211648 | bytes 327919808 | solution.py:126
  329.4 13.1 %fusion.254 = f32[8,512,2048]{2,1,0:T(8,128)} fusion(bf16[2048,8,16]{0,2,1:T(8,128)(2,1)S(1)} %get-tuple-element.1064, bf16[4,512,8,16]{1,3,2,0:T(8,128)(2,1)S(1)} %get-tuple-element.1063, s32[]{:T(128)S(6)} %copy.202), kind=kOutput, calls=%fused_computation.81.clone.1 | convolution fusion | flops 268435456 | bytes 34209796 | tf_op jit(solution)/shard_map/while/body/eval_jaxpr/ihd,jhd->hij/dot_general | solution.py:96
  342.6 24.8 %multiply_reduce_fusion.19 = (f32[8,512]{1,0:T(8,128)S(1)}, f32[8,512,2048]{2,1,0:T(8,128)}) fusion(f32[8,512,2048]{2,1,0:T(8,128)} %fusion.254, f32[8,512]{1,0:T(8,128)S(1)} %dynamic-slice_bitcast_fusion.4, bf16[2048,8,16]{0,2,1:T(8,128)(2,1)S(1)} %get-tuple-element.1061, bf16[4,512,8,16]{1,3,2,0:T(8,128)(2,1)S(1)} %get-tuple-element.1057, ...), kind=kOutput, calls=%fused_computation.69.clone.1 | convolution fusion | flops 310374400 | bytes 68845568 | tf_op jit(solution)/shard_map/while/body/eval_jaxpr/ihd,jhd->hij/dot_general | solution.py:46
  367.3 27.4 %multiply_convert_fusion.12 = bf16[8,512,2048]{2,1,0:T(8,128)(2,1)} fusion(f32[8,512,2048]{2,1,0:T(8,128)} %get-tuple-element.949, f32[8,512,2048]{2,1,0:T(8,128)} %fusion.254, f32[8,512]{1,0:T(8,128)S(1)} %get-tuple-element.950), kind=kLoop, calls=%fused_computation.68.clone.1 | loop fusion | flops 25165824 | bytes 83902464 | tf_op jit(solution)/shard_map/while/body/eval_jaxpr/convert_element_type | solution.py:108
  394.7 13.9 %fusion.256 = f32[2048,8,16]{0,2,1:T(8,128)} fusion(f32[8,512,2048]{2,1,0:T(8,128)} %get-tuple-element.949, f32[2048,8,16]{0,2,1:T(8,128)} %get-tuple-element.1041, pred[]{:T(512)S(6)} %compare.6, bf16[4,512,8,16]{1,3,2,0:T(8,128)(2,1)S(1)} %get-tuple-element.1063, s32[]{:T(128)S(6)} %copy.202), kind=kOutput, calls=%fused_computation.78.clone.1 | convolution fusion | flops 277348352 | bytes 35782660 | tf_op jit(solution)/shard_map/while/body/eval_jaxpr/hij,ihd->jhd/dot_general | solution.py:99
  408.6 8.2 convolution_multiply_fusion.6
  424.5 13.1 %fusion.254 = f32[8,512,2048]{2,1,0:T(8,128)} fusion(bf16[2048,8,16]{0,2,1:T(8,128)(2,1)S(1)} %get-tuple-element.1064, bf16[4,512,8,16]{1,3,2,0:T(8,128)(2,1)S(1)} %get-tuple-element.1063, s32[]{:T(128)S(6)} %copy.202), kind=kOutput, calls=%fused_computation.81.clone.1 | convolution fusion | flops 268435456 | bytes 34209796 | tf_op jit(solution)/shard_map/while/body/eval_jaxpr/ihd,jhd->hij/dot_general | solution.py:96
  437.6 24.8 %multiply_reduce_fusion.19 = (f32[8,512]{1,0:T(8,128)S(1)}, f32[8,512,2048]{2,1,0:T(8,128)}) fusion(f32[8,512,2048]{2,1,0:T(8,128)} %fusion.254, f32[8,512]{1,0:T(8,128)S(1)} %dynamic-slice_bitcast_fusion.4, bf16[2048,8,16]{0,2,1:T(8,128)(2,1)S(1)} %get-tuple-element.1061, bf16[4,512,8,16]{1,3,2,0:T(8,128)(2,1)S(1)} %get-tuple-element.1057, ...), kind=kOutput, calls=%fused_computation.69.clone.1 | convolution fusion | flops 310374400 | bytes 68845568 | tf_op jit(solution)/shard_map/while/body/eval_jaxpr/ihd,jhd->hij/dot_general | solution.py:46
  462.4 27.4 %multiply_convert_fusion.12 = bf16[8,512,2048]{2,1,0:T(8,128)(2,1)} fusion(f32[8,512,2048]{2,1,0:T(8,128)} %get-tuple-element.949, f32[8,512,2048]{2,1,0:T(8,128)} %fusion.254, f32[8,512]{1,0:T(8,128)S(1)} %get-tuple-element.950), kind=kLoop, calls=%fused_computation.68.clone.1 | loop fusion | flops 25165824 | bytes 83902464 | tf_op jit(solution)/shard_map/while/body/eval_jaxpr/convert_element_type | solution.py:108
  489.7 14.2 %fusion.256 = f32[2048,8,16]{0,2,1:T(8,128)} fusion(f32[8,512,2048]{2,1,0:T(8,128)} %get-tuple-element.949, f32[2048,8,16]{0,2,1:T(8,128)} %get-tuple-element.1041, pred[]{:T(512)S(6)} %compare.6, bf16[4,512,8,16]{1,3,2,0:T(8,128)(2,1)S(1)} %get-tuple-element.1063, s32[]{:T(128)S(6)} %copy.202), kind=kOutput, calls=%fused_computation.78.clone.1 | convolution fusion | flops 277348352 | bytes 35782660 | tf_op jit(solution)/shard_map/while/body/eval_jaxpr/hij,ihd->jhd/dot_general | solution.py:99
  503.9 8.2 convolution_multiply_fusion.6
  519.8 13.1 %fusion.254 = f32[8,512,2048]{2,1,0:T(8,128)} fusion(bf16[2048,8,16]{0,2,1:T(8,128)(2,1)S(1)} %get-tuple-element.1064, bf16[4,512,8,16]{1,3,2,0:T(8,128)(2,1)S(1)} %get-tuple-element.1063, s32[]{:T(128)S(6)} %copy.202), kind=kOutput, calls=%fused_computation.81.clone.1 | convolution fusion | flops 268435456 | bytes 34209796 | tf_op jit(solution)/shard_map/while/body/eval_jaxpr/ihd,jhd->hij/dot_general | solution.py:96
  532.9 24.8 %multiply_reduce_fusion.19 = (f32[8,512]{1,0:T(8,128)S(1)}, f32[8,512,2048]{2,1,0:T(8,128)}) fusion(f32[8,512,2048]{2,1,0:T(8,128)} %fusion.254, f32[8,512]{1,0:T(8,128)S(1)} %dynamic-slice_bitcast_fusion.4, bf16[2048,8,16]{0,2,1:T(8,128)(2,1)S(1)} %get-tuple-element.1061, bf16[4,512,8,16]{1,3,2,0:T(8,128)(2,1)S(1)} %get-tuple-element.1057, ...), kind=kOutput, calls=%fused_computation.69.clone.1 | convolution fusion | flops 310374400 | bytes 68845568 | tf_op jit(solution)/shard_map/while/body/eval_jaxpr/ihd,jhd->hij/dot_general | solution.py:46
  557.7 27.4 %multiply_convert_fusion.12 = bf16[8,512,2048]{2,1,0:T(8,128)(2,1)} fusion(f32[8,512,2048]{2,1,0:T(8,128)} %get-tuple-element.949, f32[8,512,2048]{2,1,0:T(8,128)} %fusion.254, f32[8,512]{1,0:T(8,128)S(1)} %get-tuple-element.950), kind=kLoop, calls=%fused_computation.68.clone.1 | loop fusion | flops 25165824 | bytes 83902464 | tf_op jit(solution)/shard_map/while/body/eval_jaxpr/convert_element_type | solution.py:108
  585.1 14.2 %fusion.256 = f32[2048,8,16]{0,2,1:T(8,128)} fusion(f32[8,512,2048]{2,1,0:T(8,128)} %get-tuple-element.949, f32[2048,8,16]{0,2,1:T(8,128)} %get-tuple-element.1041, pred[]{:T(512)S(6)} %compare.6, bf16[4,512,8,16]{1,3,2,0:T(8,128)(2,1)S(1)} %get-tuple-element.1063, s32[]{:T(128)S(6)} %copy.202), kind=kOutput, calls=%fused_computation.78.clone.1 | convolution fusion | flops 277348352 | bytes 35782660 | tf_op jit(solution)/shard_map/while/body/eval_jaxpr/hij,ihd->jhd/dot_general | solution.py:99
  599.2 8.2 convolution_multiply_fusion.6
  615.1 13.1 %fusion.254 = f32[8,512,2048]{2,1,0:T(8,128)} fusion(bf16[2048,8,16]{0,2,1:T(8,128)(2,1)S(1)} %get-tuple-element.1064, bf16[4,512,8,16]{1,3,2,0:T(8,128)(2,1)S(1)} %get-tuple-element.1063, s32[]{:T(128)S(6)} %copy.202), kind=kOutput, calls=%fused_computation.81.clone.1 | convolution fusion | flops 268435456 | bytes 34209796 | tf_op jit(solution)/shard_map/while/body/eval_jaxpr/ihd,jhd->hij/dot_general | solution.py:96
  628.2 24.8 %multiply_reduce_fusion.19 = (f32[8,512]{1,0:T(8,128)S(1)}, f32[8,512,2048]{2,1,0:T(8,128)}) fusion(f32[8,512,2048]{2,1,0:T(8,128)} %fusion.254, f32[8,512]{1,0:T(8,128)S(1)} %dynamic-slice_bitcast_fusion.4, bf16[2048,8,16]{0,2,1:T(8,128)(2,1)S(1)} %get-tuple-element.1061, bf16[4,512,8,16]{1,3,2,0:T(8,128)(2,1)S(1)} %get-tuple-element.1057, ...), kind=kOutput, calls=%fused_computation.69.clone.1 | convolution fusion | flops 310374400 | bytes 68845568 | tf_op jit(solution)/shard_map/while/body/eval_jaxpr/ihd,jhd->hij/dot_general | solution.py:46
  653.0 27.4 %multiply_convert_fusion.12 = bf16[8,512,2048]{2,1,0:T(8,128)(2,1)} fusion(f32[8,512,2048]{2,1,0:T(8,128)} %get-tuple-element.949, f32[8,512,2048]{2,1,0:T(8,128)} %fusion.254, f32[8,512]{1,0:T(8,128)S(1)} %get-tuple-element.950), kind=kLoop, calls=%fused_computation.68.clone.1 | loop fusion | flops 25165824 | bytes 83902464 | tf_op jit(solution)/shard_map/while/body/eval_jaxpr/convert_element_type | solution.py:108
  680.4 14.2 %fusion.256 = f32[2048,8,16]{0,2,1:T(8,128)} fusion(f32[8,512,2048]{2,1,0:T(8,128)} %get-tuple-element.949, f32[2048,8,16]{0,2,1:T(8,128)} %get-tuple-element.1041, pred[]{:T(512)S(6)} %compare.6, bf16[4,512,8,16]{1,3,2,0:T(8,128)(2,1)S(1)} %get-tuple-element.1063, s32[]{:T(128)S(6)} %copy.202), kind=kOutput, calls=%fused_computation.78.clone.1 | convolution fusion | flops 277348352 | bytes 35782660 | tf_op jit(solution)/shard_map/while/body/eval_jaxpr/hij,ihd->jhd/dot_general | solution.py:99
  694.6 8.2 convolution_multiply_fusion.6
  755.1 84.7 %while.57 = (s32[]{:T(128)}, f32[1024,8,16]{0,2,1:T(8,128)S(1)}, f32[1024,8,16]{0,2,1:T(8,128)}, bf16[2,512,128]{2,1,0:T(8,128)(2,1)}, bf16[2,512,8,16]{1,3,2,0:...) while((s32[]{:T(128)}, f32[1024,8,16]{0,2,1:T(8,128)S(1)}, ...), condition=%wide.region_32.33_spmd.clone, body=%wide.region_30.32_spmd.clone.sunk | while | flops 710669312 | bytes 138379600 | solution.py:126
  757.6 8.1 fusion.266
  765.7 9.6 multiply_reduce_fusion.20
  775.3 9.5 multiply_convert_fusion.13
  799.8 8.1 fusion.266
  807.9 9.6 multiply_reduce_fusion.20
  817.5 9.5 multiply_convert_fusion.13
  862.2 41.1 %all-reduce = (f32[2,256]{1,0:T(2,128)}, f32[2,2,128]{2,1,0:T(2,128)}, f32[2,4,128]{2,1,0:T(4,128)}) all-reduce(f32[2,256]{1,0:T(2,128)S(1)} %pad_maximum_fusion.12, f32[2,2,128]{2,1,0:T(2,128)S(1)} %pad_maximum_fusion.13, f32[2,4,128]{2,1,0:T(4,128)S(1)} %pad_maximum_fusion.11), channel_id=1, replica_groups=mesh['strip'=8,'sub'=4] {'strip','sub'}, use_global_device_ids=true, to_apply=%region_39.40 | all-reduce | flops 2048 | bytes 16384 | tf_op jit(solution)/shard_map/psum | solution.py:300
  903.3 91.1 %all-reduce.4.cloned.1.call-done = (f32[2,128,384]{2,1,0:T(8,128)}, f32[2,128,128]{2,1,0:T(8,128)}, f32[2,128,256]{2,1,0:T(8,128)}, f32[2,256,128]{2,1,0:T(8,128)}) async-done(((f32[2,128,384]{2,1,0:T(8,128)}, f32[2,128,128]{2,1,0:T(8,128)}, f32[2,128,256]{2,1,0:T(8,128)}, f32[2,256,128]{2,1,0:T(8,128)}), (f32[2,128,384]{2,1,0:T(8,128)}, f32[2,128,128]{2,1,0:T(8,128)}, f32[2,128,256]{2,1,0:T(8,128)}, ...) | async-done | bytes 1048592 | tf_op jit(solution)/shard_map/psum | solution.py:300
  (423 shorter events, 243.0 us)
Async XLA Ops:
  13.7 51.0 %all-to-all-start.1 = ((s32[8,256,2]{1,2,0:T(2,128)}), s32[8,256,2]{1,2,0:T(2,128)}, u32[]{:S(2)}, u32[]{:S(2)}) async-start(s32[8,256,2]{1,2,0:T(2,128)} %copy.100), calls=%async_computation.1 | async-start | bytes 32768 | tf_op jit(solution)/shard_map/all_to_all | solution.py:279
  28.9 28.7 %copy-start.28 = (bf16[1024,128]{0,1:T(8,128)(2,1)S(1)}, bf16[1024,128]{0,1:T(8,128)(2,1)}, u32[]{:S(2)}) copy-start(bf16[1024,128]{0,1:T(8,128)(2,1)} %copy-done.27) | copy-start | bytes 786436
  29.0 28.7 %copy-start.45 = (bf16[2,128,128]{2,1,0:T(8,128)(2,1)S(1)}, bf16[2,128,128]{2,1,0:T(8,128)(2,1)}, u32[]{:S(2)}) copy-start(bf16[2,128,128]{2,1,0:T(8,128)(2,1)} %param.27) | copy-start | bytes 196612
  29.0 29.2 %copy-start.43 = (bf16[2,128,256]{2,1,0:T(8,128)(2,1)S(1)}, bf16[2,128,256]{2,1,0:T(8,128)(2,1)}, u32[]{:S(2)}) copy-start(bf16[2,128,256]{2,1,0:T(8,128)(2,1)} %param.28) | copy-start | bytes 393220
  29.0 29.2 %copy-start.75 = (f32[1,256]{1,0:T(1,128)S(1)}, f32[1,256]{1,0:T(1,128)}, u32[]{:S(2)}) copy-start(f32[1,256]{1,0:T(1,128)} %get-tuple-element.674) | copy-start | bytes 3076
  29.0 29.8 %copy-start.89 = (bf16[2,256,128]{2,1,0:T(8,128)(2,1)S(1)}, bf16[2,256,128]{2,1,0:T(8,128)(2,1)}, u32[]{:S(2)}) copy-start(bf16[2,256,128]{2,1,0:T(8,128)(2,1)} %param.29) | copy-start | bytes 393220
  29.0 31.3 %copy-start.35 = (bf16[1,1024,128]{2,1,0:T(8,128)(2,1)S(1)}, bf16[1,1024,128]{2,1,0:T(8,128)(2,1)}, u32[]{:S(2)}) copy-start(bf16[1,1024,128]{2,1,0:T(8,128)(2,1)} %get-tuple-element.656) | copy-start | bytes 786436
  29.0 85.2 %copy-start.36 = (bf16[2,128,384]{2,1,0:T(8,128)(2,1)S(1)}, bf16[2,128,384]{2,1,0:T(8,128)(2,1)}, u32[]{:S(2)}) copy-start(bf16[2,128,384]{2,1,0:T(8,128)(2,1)} %param.26) | copy-start | bytes 589828
  56.9 63.3 %copy-start.1 = (bf16[1024,8,16]{0,2,1:T(8,128)(2,1)}, bf16[1024,8,16]{0,2,1:T(8,128)(2,1)S(1)}, u32[]{:S(2)}) copy-start(bf16[1024,8,16]{0,2,1:T(8,128)(2,1)S(1)} %get-tuple-element.1127) | copy-start | bytes 786436
  56.9 63.3 %copy-start.7 = (bf16[2,512,8,16]{1,3,2,0:T(8,128)(2,1)}, bf16[2,512,8,16]{1,3,2,0:T(8,128)(2,1)S(1)}, u32[]{:S(2)}) copy-start(bf16[2,512,8,16]{1,3,2,0:T(8,128)(2,1)S(1)} %get-tuple-element.1129) | copy-start | bytes 786436
  56.9 63.3 %copy-start.15 = (bf16[1024,8,16]{0,2,1:T(8,128)(2,1)}, bf16[1024,8,16]{0,2,1:T(8,128)(2,1)S(1)}, u32[]{:S(2)}) copy-start(bf16[1024,8,16]{0,2,1:T(8,128)(2,1)S(1)} %get-tuple-element.1132) | copy-start | bytes 786436
  57.7 30.9 %copy-start.67 = (f32[128]{0:T(128)}, f32[128]{0:T(128)S(1)}, u32[]{:S(2)}) copy-start(f32[128]{0:T(128)S(1)} %get-tuple-element.690) | copy-start | bytes 1540
  57.7 30.9 %copy-start.73 = (f32[128]{0:T(128)}, f32[128]{0:T(128)S(1)}, u32[]{:S(2)}) copy-start(f32[128]{0:T(128)S(1)} %get-tuple-element.666) | copy-start | bytes 1540
  57.7 62.5 %copy-start.72 = (f32[128]{0:T(128)}, f32[128]{0:T(128)S(1)}, u32[]{:S(2)}) copy-start(f32[128]{0:T(128)S(1)} %get-tuple-element.692) | copy-start | bytes 1540
  57.7 62.6 %copy-start.69 = (f32[128]{0:T(128)}, f32[128]{0:T(128)S(1)}, u32[]{:S(2)}) copy-start(f32[128]{0:T(128)S(1)} %get-tuple-element.691) | copy-start | bytes 1540
  59.6 55.0 %copy-start.19 = (f32[1024,128]{0,1:T(8,128)}, f32[1024,128]{0,1:T(8,128)S(1)}, u32[]{:S(2)}) copy-start(f32[1024,128]{0,1:T(8,128)S(1)} %get-tuple-element.678) | copy-start | bytes 1572868
  64.7 20.2 %all-to-all-start.3 = ((bf16[8,256,128]{2,1,0:T(8,128)(2,1)}), bf16[8,256,128]{2,1,0:T(8,128)(2,1)S(1)}, u32[]{:S(2)}, u32[]{:S(2)}) async-start(bf16[8,256,128]{2,1,0:T(8,128)(2,1)} %bitcast.52), calls=%async_computation.3 | async-start | bytes 1048576 | tf_op jit(solution)/shard_map/all_to_all | solution.py:281
  84.9 29.2 %copy-start.21 = (bf16[8,256,128]{2,1,0:T(8,128)(2,1)}, bf16[8,256,128]{2,1,0:T(8,128)(2,1)S(1)}, u32[]{:S(2)}) copy-start(bf16[8,256,128]{2,1,0:T(8,128)(2,1)S(1)} %all-to-all-done.3) | copy-start | bytes 1572868
  84.9 29.2 %all-to-all-start = ((bf16[8,256,256]{2,1,0:T(8,128)(2,1)}), bf16[8,256,256]{2,1,0:T(8,128)(2,1)S(1)}, u32[]{:S(2)}, u32[]{:S(2)}) async-start(bf16[8,256,256]{2,1,0:T(8,128)(2,1)} %bitcast.393), calls=%async_computation | async-start | bytes 2097152 | tf_op jit(solution)/shard_map/all_to_all | solution.py:272
  120.2 181.6 %copy-start.46 = (bf16[2,128,128]{2,1,0:T(8,128)(2,1)S(1)}, bf16[2,128,128]{2,1,0:T(8,128)(2,1)}, u32[]{:S(2)}) copy-start(bf16[2,128,128]{2,1,0:T(8,128)(2,1)} %param.27) | copy-start | bytes 196612
  120.2 181.6 %copy-start.80 = (f32[128]{0:T(128)S(1)}, f32[128]{0:T(128)}, u32[]{:S(2)}) copy-start(f32[128]{0:T(128)} %get-tuple-element.663) | copy-start | bytes 1540
  120.2 184.0 %copy-start.44 = (bf16[2,128,256]{2,1,0:T(8,128)(2,1)S(1)}, bf16[2,128,256]{2,1,0:T(8,128)(2,1)}, u32[]{:S(2)}) copy-start(bf16[2,128,256]{2,1,0:T(8,128)(2,1)} %param.28) | copy-start | bytes 393220
  120.2 184.0 %copy-start.65 = (f32[128]{0:T(128)S(1)}, f32[128]{0:T(128)}, u32[]{:S(2)}) copy-start(f32[128]{0:T(128)} %get-tuple-element.689) | copy-start | bytes 1540
  120.2 184.0 %copy-start.74 = (f32[128]{0:T(128)S(1)}, f32[128]{0:T(128)}, u32[]{:S(2)}) copy-start(f32[128]{0:T(128)} %get-tuple-element.662) | copy-start | bytes 1540
  120.2 188.2 %copy-start.22 = (bf16[8,256,128]{2,1,0:T(8,128)(2,1)S(1)}, bf16[8,256,128]{2,1,0:T(8,128)(2,1)}, u32[]{:S(2)}) copy-start(bf16[8,256,128]{2,1,0:T(8,128)(2,1)} %copy-done.21) | copy-start | bytes 1572868
  120.2 188.2 %copy-start.57 = (f32[2048,1]{0,1:T(1,128)S(1)}, f32[2048,1]{0,1:T(1,128)}, u32[]{:S(2)}) copy-start(f32[2048,1]{0,1:T(1,128)} %get-tuple-element.657) | copy-start | bytes 24580
  327.1 401.4 %copy-start.42 = (f32[2048]{0:T(1024)S(1)}, f32[2048]{0:T(1024)}, u32[]{:S(2)}) copy-start(f32[2048]{0:T(1024)} %copy-done.41) | copy-start | bytes 24580
  327.1 401.4 %copy-start.50 = (f32[2048]{0:T(1024)S(1)}, f32[2048]{0:T(1024)}, u32[]{:S(2)}) copy-start(f32[2048]{0:T(1024)} %copy-done.49) | copy-start | bytes 24580
  708.8 41.9 %copy-start.13 = (f32[1024,128]{0,1:T(8,128)S(1)}, f32[1024,128]{0,1:T(8,128)}, u32[]{:S(2)}) copy-start(f32[1024,128]{0,1:T(8,128)} %copy-done.12) | copy-start | bytes 1572868
  713.1 31.0 %copy-start.56 = (f32[1024]{0:T(1024)S(1)}, f32[1024]{0:T(1024)}, u32[]{:S(2)}) copy-start(f32[1024]{0:T(1024)} %copy-done.55) | copy-start | bytes 12292
  713.1 31.0 %copy-start.61 = (f32[1024]{0:T(1024)S(1)}, f32[1024]{0:T(1024)}, u32[]{:S(2)}) copy-start(f32[1024]{0:T(1024)} %copy-done.60) | copy-start | bytes 12292
  713.1 31.1 %copy-start.63 = (f32[1024]{0:T(1024)S(1)}, f32[1024]{0:T(1024)}, u32[]{:S(2)}) copy-start(f32[1024]{0:T(1024)} %copy-done.62) | copy-start | bytes 12292
  713.1 31.1 %copy-start.70 = (f32[128]{0:T(128)S(1)}, f32[128]{0:T(128)}, u32[]{:S(2)}) copy-start(f32[128]{0:T(128)} %copy-done.69) | copy-start | bytes 1540
  713.1 39.7 %copy-start.54 = (f32[1024]{0:T(1024)S(1)}, f32[1024]{0:T(1024)}, u32[]{:S(2)}) copy-start(f32[1024]{0:T(1024)} %copy-done.53) | copy-start | bytes 12292
  713.1 39.7 %copy-start.59 = (f32[1024]{0:T(1024)S(1)}, f32[1024]{0:T(1024)}, u32[]{:S(2)}) copy-start(f32[1024]{0:T(1024)} %copy-done.58) | copy-start | bytes 12292
  713.1 39.7 %copy-start.68 = (f32[128]{0:T(128)S(1)}, f32[128]{0:T(128)}, u32[]{:S(2)}) copy-start(f32[128]{0:T(128)} %copy-done.67) | copy-start | bytes 1540
  713.1 40.5 %copy-start.47 = (bf16[2,128,128]{2,1,0:T(8,128)(2,1)S(1)}, bf16[2,128,128]{2,1,0:T(8,128)(2,1)}, u32[]{:S(2)}) copy-start(bf16[2,128,128]{2,1,0:T(8,128)(2,1)} %param.27) | copy-start | bytes 196612
  716.5 38.5 %copy-start.2 = (bf16[1024,8,16]{0,2,1:T(8,128)(2,1)S(1)}, bf16[1024,8,16]{0,2,1:T(8,128)(2,1)}, u32[]{:S(2)}) copy-start(bf16[1024,8,16]{0,2,1:T(8,128)(2,1)} %copy-done.1) | copy-start | bytes 786436
  716.5 38.5 %copy-start.3 = (f32[1024,8,16]{0,2,1:T(8,128)S(1)}, f32[1024,8,16]{0,2,1:T(8,128)}, u32[]{:S(2)}) copy-start(f32[1024,8,16]{0,2,1:T(8,128)} %custom-call.2) | copy-start | bytes 1572868
  716.5 38.5 %copy-start.8 = (bf16[2,512,8,16]{1,3,2,0:T(8,128)(2,1)S(1)}, bf16[2,512,8,16]{1,3,2,0:T(8,128)(2,1)}, u32[]{:S(2)}) copy-start(bf16[2,512,8,16]{1,3,2,0:T(8,128)(2,1)} %copy-done.7) | copy-start | bytes 786436
  716.5 38.5 %copy-start.16 = (bf16[1024,8,16]{0,2,1:T(8,128)(2,1)S(1)}, bf16[1024,8,16]{0,2,1:T(8,128)(2,1)}, u32[]{:S(2)}) copy-start(bf16[1024,8,16]{0,2,1:T(8,128)(2,1)} %copy-done.15) | copy-start | bytes 786436
  716.5 38.5 %copy-start.38 = (s32[1024]{0:T(1024)S(1)}, s32[1024]{0:T(1024)}, u32[]{:S(2)}) copy-start(s32[1024]{0:T(1024)} %get-tuple-element.1162) | copy-start | bytes 12292
  716.5 38.5 %copy-start.40 = (s32[1024]{0:T(1024)S(1)}, s32[1024]{0:T(1024)}, u32[]{:S(2)}) copy-start(s32[1024]{0:T(1024)} %get-tuple-element.1164) | copy-start | bytes 12292
  718.5 18.1 %all-to-all-start.4 = ((bf16[8,256,128]{2,1,0:T(8,128)(2,1)}), bf16[8,256,128]{2,1,0:T(8,128)(2,1)S(1)}, u32[]{:S(2)}, u32[]{:S(2)}) async-start(bf16[8,256,128]{2,1,0:T(8,128)(2,1)} %bitcast.405), calls=%async_computation.4 | async-start | bytes 1048576 | tf_op jit(solution)/shard_map/all_to_all | solution.py:293
  736.5 111.0 %all-to-all-start.2 = ((bf16[8,256,128]{2,1,0:T(8,128)(2,1)}), bf16[8,256,128]{2,1,0:T(8,128)(2,1)}, u32[]{:S(2)}, u32[]{:S(2)}) async-start(bf16[8,256,128]{2,1,0:T(8,128)(2,1)} %bitcast.401), calls=%async_computation.2 | async-start | bytes 1048576 | tf_op jit(solution)/shard_map/all_to_all | solution.py:292
  740.7 253.7 %all-reduce.4.cloned.1.call-start = ((), (), s32[]{:S(2)}) async-start(), calls=%async_computation.5 | async-start | bytes 2097152 | tf_op jit(solution)/shard_map/psum | solution.py:300
  755.0 86.5 %copy-start.14 = (f32[1024,128]{0,1:T(8,128)S(1)}, f32[1024,128]{0,1:T(8,128)}, u32[]{:S(2)}) copy-start(f32[1024,128]{0,1:T(8,128)} %copy-done.12) | copy-start | bytes 1572868
  755.0 99.1 %copy-start.26 = (bf16[1024,128]{1,0:T(8,128)(2,1)S(1)}, bf16[1024,128]{1,0:T(8,128)(2,1)}, u32[]{:S(2)}) copy-start(bf16[1024,128]{1,0:T(8,128)(2,1)} %param.23) | copy-start | bytes 786436
  (57 other events, 715.8 us)
Sparse Core Ops, SparseCore 0:
  862.1 132.2 all-reduce.3
where the time goes:
time: 1020 us; the launch traced here: 1010 us
  matrix products  478 us (47%)
  other arithmetic  243 us (24%)
  waiting for transfers between devices  121 us (12%)
  local copies, waits for them, and re-layouts  83.3 us (8%)
  blocking collectives  41.1 us (4%)
  starting transfers between devices  24.8 us (2%)
  between operations  16 us (2%)
    dot_general x12, matrix products, block_scores(): jnp.einsum('ihd,jhd->hij', query_blk, head_keys, preferred_element_type=j...  178 us
    convert_element_type x6, other arithmetic, one_block(): score_grad = score_grad.astype(jnp.bfloat16)  129 us
    psum x1, waiting for transfers between devices, local(): totals = lax.psum(stacked, ('strip', 'sub'))  91.1 us
    dot_general x6, matrix products, one_block(): jnp.einsum('ihd,jhd->hij', grad_blk, head_values, preferred_element_type=...  68.7 us
    reduce_sum x6, other arithmetic, one_block(): summed = jnp.sum(exponent, axis=-1, keepdims=True)  68.4 us
    dot_general x6, matrix products, one_block(): jnp.einsum('hij,jhd->ihd', attention, head_values, preferred_element_type...  64.4 us
    dot_general x6, matrix products, one_block(): jnp.einsum('hij,ihd->jhd', attention.astype(jnp.bfloat16), grad_blk, pref...  58.8 us
    dot_general x6, matrix products, one_block(): jnp.einsum('hij,jhd->ihd', score_grad, head_keys, preferred_element_type=...  44.6 us
  transfers between devices with their start and end apart: 6, of which 4 were waited for; matrix products, arithmetic and copies ran while one was open for 17% of the time, Pallas kernels for 0%

commit v1 on v0

v1 whole, which is shorter than its diff:
```python
import functools

import jax
import jax.numpy as jnp
from jax import lax
from jax.experimental import pallas as pl
from jax.experimental.pallas import tpu as pltpu
from jax.sharding import PartitionSpec as P

HEADS = 8
EPS = 1e-05
NEGATIVE = -1e30
BLK = 128
CH = 256
WINDOWS = 64
VMEM = 60 * 1024 * 1024
F32, BF16, I32 = jnp.float32, jnp.bfloat16, jnp.int32
GRAD_ROWS = 1040


def dot(a, b):
    return lax.dot_general(a, b, (((1,), (0,)), ((), ())), preferred_element_type=F32)


def dot_nt(a, b):
    return lax.dot_general(a, b, (((1,), (1,)), ((), ())), preferred_element_type=F32)


def flip(x):
    return jnp.transpose(x.astype(F32)).astype(BF16)


def iota(shape, dim):
    return lax.broadcasted_iota(I32, shape, dim)


def column(row):
    return jnp.transpose(jnp.broadcast_to(row, (BLK, BLK)))


def twice(x):
    return jnp.concatenate([x, x], axis=1)


def seat_rows(win, live, cnt_ref, start_ref, pcol_ref):
    total = win.shape[1]
    blocks = total // BLK
    key = jnp.where(live, win, -1)
    hot = (iota((WINDOWS, total), 0) == key).astype(F32)
    hot_low = hot.astype(BF16)
    stacked = jnp.concatenate([hot_low[:, b * BLK : (b + 1) * BLK] for b in range(blocks)], axis=0)
    row_at, col_at = iota((BLK, 2 * BLK), 0), iota((BLK, 2 * BLK), 1)
    counter = ((row_at < col_at) | (col_at >= BLK)).astype(F32).astype(BF16)
    sums = dot(stacked, counter)
    carry = jnp.zeros((WINDOWS, BLK), F32)
    before = []
    for b in range(blocks):
        part = sums[b * WINDOWS : (b + 1) * WINDOWS]
        before.append(part[:, :BLK] + carry)
        carry = carry + part[:, BLK:]
    counts = carry.astype(I32)
    cnt_ref[...] = counts
    cursor = jnp.zeros((8, BLK), I32)
    room = jnp.zeros((8, BLK), I32)
    largest = jnp.zeros((8, BLK), I32)
    sub = iota((8, BLK), 0)
    for g in range(WINDOWS // 8):
        tile = jnp.zeros((8, BLK), I32)
        for i in range(8):
            w = 8 * g + i
            count = jnp.broadcast_to(counts[w : w + 1, :], (8, BLK))
            fits = count <= room
            start = jnp.where(fits, cursor, cursor + room)
            tile = jnp.where(sub == i, start, tile)
            cursor = start + count
            room = jnp.where(fits, room - count, (-count) & (BLK - 1))
            largest = jnp.maximum(largest, count)
        start_ref[8 * g : 8 * g + 8, :] = tile
    starts = start_ref[...].astype(F32)
    for b in range(blocks):
        sl = slice(b * BLK, (b + 1) * BLK)
        seat = jnp.sum(hot[:, sl] * (before[b] + starts), axis=0, keepdims=True)
        seat = jnp.where(live[:, sl], seat, -1.0)
        pcol_ref[sl, :] = column(seat).astype(I32)
    used = (jnp.max(cursor) + (BLK - 1)) // BLK
    return used, jnp.max(largest)


def norm_forward(hidden, gain, shift):
    size = hidden.shape[0]
    average = jnp.sum(hidden, axis=0, keepdims=True) * (1.0 / size)
    centered = hidden - average
    inverse = lax.rsqrt(jnp.sum(centered * centered, axis=0, keepdims=True) * (1.0 / size) + EPS)
    normed = centered * inverse
    return normed * gain + shift, normed, inverse


def norm_backward(upstream, normed, inverse, gain):
    size = upstream.shape[0]
    scaled = upstream * gain
    center = jnp.sum(scaled, axis=0, keepdims=True) * (1.0 / size)
    along = jnp.sum(scaled * normed, axis=0, keepdims=True) * (1.0 / size)
    return inverse * (scaled - center - normed * along)


GELU_A = 0.7978845608028654
GELU_B = 0.044715


def tiles(x):
    return x.reshape(x.shape[0] // 8, 8, x.shape[1])


def own_heads(x):
    size = x.shape[0] // HEADS
    return jnp.concatenate(
        [x[h * size : (h + 1) * size, h * BLK : (h + 1) * BLK] for h in range(HEADS)], axis=0
    )


def whole_rows(x):
    return jnp.broadcast_to(x, (8, x.shape[1]))


def head_stack(x):
    size = x.shape[0] // HEADS
    zero = jnp.zeros((size, x.shape[1]), x.dtype)
    blocks = []
    for h in range(HEADS):
        rows = [zero] * HEADS
        rows[h] = x[h * size : (h + 1) * size]
        blocks.append(jnp.concatenate(rows, axis=0))
    return jnp.concatenate(blocks, axis=1)


def layer_kernel(mode, level, cap, *refs):
    refs = list(refs)
    take = lambda n: [refs.pop(0) for _ in range(n)]
    if mode == "mid":
        meta_ref, rest_ref, x_ref = take(3)
    else:
        meta_ref, x_ref, pos_ref = take(3)
        if mode == "bwd":
            (grad_ref,) = take(1)
    wqkv_ref, wout_ref, wup_ref, wdown_ref, bup_ref, gains_ref, shifts_ref = take(7)
    if mode == "fwd":
        (msg_ref,) = take(1)
    else:
        back_ref, wg_ref = take(2)
    (
        cnt_ref, start_ref, pcol_ref, srct_ref, pick_ref, acc_ref,
        wqkvt_ref, woutt_ref, wupt_ref, wdownt_ref, cols_ref,
        xt_ref, ut_ref, qt_ref, kt_ref, vt_ref, k_ref, v_ref, idrow_ref, idcol_ref, place_ref,
    ) = take(21)
    if mode != "fwd":
        (
            dy_ref, yt_ref, dh_ref, dq_ref, dk_ref, dv_ref, a_ref,
            gq_ref, go_ref, gu_ref, gd_ref, gg_ref,
        ) = take(12)
        if mode == "bwd":
            (rowst_ref,) = take(1)
    stat_ref, stack_ref, span_ref = take(3)

    total = meta_ref.shape[1]
    width = x_ref.shape[-1]
    head = width // HEADS
    scale = head ** (-0.5)
    meta = meta_ref[...].astype(I32)
    win, live = meta[0:1], meta[1:2] > 0

    used, largest = seat_rows(win, live, cnt_ref, start_ref, pcol_ref)
    chunks = (used + 1) // 2
    several = largest > BLK

    for b in range(total // BLK):
        sl = slice(b * BLK, (b + 1) * BLK)
        if mode == "mid":
            srct_ref[0:width, sl] = flip(x_ref[sl, :])
            rest = flip(rest_ref[sl, :])
            srct_ref[width : 3 * width, sl] = rest
        else:
            srct_ref[0:width, sl] = flip(x_ref[sl, :])
            srct_ref[width : 2 * width, sl] = flip(pos_ref[0, sl, :])
    tags = srct_ref.shape[0] - 16
    at = iota((16, total), 0)
    rows = jnp.where(at == 0, win + 1, jnp.where(at == 1, 1, 0))
    if mode != "mid":
        rows = jnp.where(at == 2, meta[2:3], jnp.where(at == 3, meta[3:4], rows))
    srct_ref[tags:, :] = rows.astype(F32).astype(BF16)
    if mode == "bwd":
        for b in range(grad_ref.shape[0] // BLK):
            sl = slice(b * BLK, (b + 1) * BLK)
            rowst_ref[:, sl] = flip(grad_ref[sl, :])

    for b in range(3):
        sl = slice(b * BLK, (b + 1) * BLK)
        wqkvt_ref[sl, :] = flip(wqkv_ref[level, :, sl])
    woutt_ref[...] = flip(wout_ref[level])
    for b in range(2):
        sl = slice(b * BLK, (b + 1) * BLK)
        wupt_ref[sl, :] = flip(wup_ref[level, :, sl])
        wdownt_ref[:, sl] = flip(wdown_ref[level, sl, :])
        cols_ref[6 + b] = column(bup_ref[level : level + 1, sl])
    for b in range(2):
        cols_ref[b] = column(gains_ref[level, b : b + 1, :])
    for b in range(4):
        cols_ref[2 + b] = column(shifts_ref[level, b : b + 1, :])

    acc_ref[...] = jnp.zeros(acc_ref.shape, F32)
    if mode != "fwd":
        for ref in (gq_ref, go_ref, gu_ref, gd_ref, gg_ref):
            ref[...] = jnp.zeros(ref.shape, F32)

    @pl.loop(0, chunks)
    def _(c):
        seat = iota((BLK, BLK), 1) + c * CH
        for b in range(total // BLK):
            sl = slice(b * BLK, (b + 1) * BLK)
            col = pcol_ref[sl, :]
            for t in range(2):
                pick_ref[c, sl, t * BLK : (t + 1) * BLK] = (
                    (col == seat + t * BLK).astype(F32).astype(BF16)
                )
        moved = dot(srct_ref[...], pick_ref[c])
        xt = moved[:width]
        low = xt.astype(BF16)
        joined = (xt + moved[width : 2 * width]).astype(BF16)
        xt_ref[c] = low
        ut_ref[c] = joined
        qk = dot(wqkvt_ref[: 2 * width], joined).astype(BF16).astype(F32)
        vt = dot(wqkvt_ref[2 * width :], low).astype(BF16).astype(F32)
        qt_ref[c] = (qk[:width] * scale).astype(BF16)
        kt = qk[width:]
        ids = moved[tags : tags + 1]
        idrow_ref[c] = jnp.broadcast_to(ids, (8, CH))
        for t in range(2):
            sl = slice(t * BLK, (t + 1) * BLK)
            b = 2 * c + t
            kt_ref[b] = kt[:, sl].astype(BF16)
            vt_ref[b] = vt[:, sl].astype(BF16)
            k_ref[b] = jnp.transpose(kt[:, sl]).astype(BF16)
            v_ref[b] = jnp.transpose(vt[:, sl]).astype(BF16)
            idcol_ref[b] = column(ids[:, sl])
            if mode != "fwd":
                dk_ref[b] = jnp.zeros((BLK, width), F32)
                dv_ref[b] = jnp.zeros((BLK, width), F32)
        if mode == "mid":
            dy_ref[c] = moved[2 * width : 3 * width].astype(BF16)
        else:
            spot = moved[tags + 2 : tags + 3] * cap + moved[tags + 3 : tags + 4]
            spot = jnp.where(moved[tags + 1 : tags + 2] > 0.5, spot, -1.0)
            place_ref[c] = jnp.broadcast_to(spot, (8, CH)).astype(I32)

    @pl.when(several)
    def _():
        at = iota((WINDOWS, BLK), 1)
        count, start = cnt_ref[...], start_ref[...]
        first = lax.shift_right_logical(start, 7)
        final = lax.shift_right_logical(start + jnp.maximum(count, 1) - 1, 7)
        touch = (count > 0) & (first <= at) & (at <= final)
        low_at = jnp.min(jnp.where(touch, first, at), axis=0, keepdims=True)
        high_at = jnp.max(jnp.where(touch, final, at), axis=0, keepdims=True)
        for b in range(total // 64):
            span_ref[0, b] = jnp.max(jnp.where(at[0:1] == b, low_at, 0))
            span_ref[1, b] = jnp.max(jnp.where(at[0:1] == b, high_at, 0))

    def scores(stack, key_block, ids):
        bias = jnp.where(idcol_ref[key_block] == ids, 0.0, NEGATIVE)
        return dot(k_ref[key_block], stack), bias

    def chunk(c, single):
        qt = qt_ref[c]
        stacks, stats, mixed = [], [], []
        for t in range(2):
            sl = slice(t * BLK, (t + 1) * BLK)
            b = 2 * c + t
            ids = idrow_ref[c][0:1, sl]
            stack = head_stack(qt[:, sl])
            stacks.append(stack)
            if single:
                sc, bias = scores(stack, b, ids)
                parts = []
                for h in range(HEADS):
                    hs = slice(h * BLK, (h + 1) * BLK)
                    masked = sc[:, hs] + bias
                    top = jnp.max(masked, axis=0, keepdims=True)
                    e = jnp.exp(masked - top)
                    a = e * (1.0 / jnp.sum(e, axis=0, keepdims=True))
                    if mode != "fwd":
                        a_ref[t, :, hs] = a
                    parts.append(dot(vt_ref[b, h * head : (h + 1) * head, :], a.astype(BF16)))
                mixed.append(jnp.concatenate(parts, axis=0))
            else:
                lo, hi = span_ref[0, b], span_ref[1, b] + 1
                stack_ref[t, 0] = stack

                def masked_of(j, t=t, ids=ids):
                    sc, bias = scores(stack_ref[t, 0], j, ids)
                    return sc + jnp.concatenate([bias] * HEADS, axis=1)

                def step_top(j, top):
                    return jnp.maximum(top, jnp.max(tiles(masked_of(j)), axis=0))

                top = lax.fori_loop(lo, hi, step_top, jnp.full((8, HEADS * BLK), 2 * NEGATIVE, F32))
                stat_ref[t, 0] = whole_rows(jnp.max(top, axis=0, keepdims=True))

                def step_sum(j, summed, t=t, masked_of=masked_of):
                    top = stat_ref[t, 0]
                    return summed + jnp.sum(jnp.exp(tiles(masked_of(j)) - top[None]), axis=0)

                summed = lax.fori_loop(lo, hi, step_sum, jnp.zeros((8, HEADS * BLK), F32))
                stat_ref[t, 1] = whole_rows(1.0 / jnp.sum(summed, axis=0, keepdims=True))

                def step_mix(j, out, t=t, masked_of=masked_of):
                    top, inv = stat_ref[t, 0], stat_ref[t, 1]
                    a = jnp.exp(tiles(masked_of(j)) - top[None]) * inv[None]
                    a = a.reshape(BLK, HEADS * BLK).astype(BF16)
                    return out + own_heads(dot(vt_ref[j], a))

                mixed.append(lax.fori_loop(lo, hi, step_mix, jnp.zeros((width, BLK), F32)))
                stats.append((masked_of, lo, hi))
        mixed = jnp.concatenate(mixed, axis=1)
        mixed_low = mixed.astype(BF16)
        gain_one, gain_two = twice(cols_ref[0]), twice(cols_ref[1])
        attended = dot(woutt_ref[...], mixed_low) + twice(cols_ref[2])
        first_out, normed_one, inverse_one = norm_forward(
            xt_ref[c].astype(F32) + attended, gain_one, twice(cols_ref[3])
        )
        first_low = first_out.astype(BF16)
        bias_up = jnp.concatenate([twice(cols_ref[6]), twice(cols_ref[7])], axis=0)
        before = dot(wupt_ref[...], first_low) + bias_up
        square = before * before
        bend = jnp.tanh(GELU_A * before * (1.0 + GELU_B * square))
        activated = (0.5 * before * (1.0 + bend)).astype(BF16)
        branch = dot(wdownt_ref[...], activated) + twice(cols_ref[4])
        result, normed_two, inverse_two = norm_forward(
            first_out + branch, gain_two, twice(cols_ref[5])
        )
        if mode == "fwd":
            out_low = result.astype(BF16)
            at = iota((BLK, CH), 0)
            spot = place_ref[c][0:1]
            for r in range(acc_ref.shape[0] // BLK):
                sl = slice(r * BLK, (r + 1) * BLK)
                hot = (at + r * BLK == spot).astype(F32).astype(BF16)
                acc_ref[sl, :] += dot_nt(hot, out_low)
            return
        if mode == "mid":
            yt_ref[c] = result.astype(BF16)
            upstream = dy_ref[c].astype(F32)
        else:
            at = iota((BLK, CH), 0)
            spot = place_ref[c][0:1]
            hot = jnp.concatenate(
                [
                    (at + r * BLK == spot).astype(F32).astype(BF16)
                    for r in range(rowst_ref.shape[1] // BLK)
                ],
                axis=0,
            )
            upstream = dot(rowst_ref[...], hot)
        ones = jnp.ones((16, CH), BF16)
        gg_ref[0] += upstream * normed_two
        gg_ref[1] += upstream
        second = norm_backward(upstream, normed_two, inverse_two, gain_two)
        branch_low = second.astype(BF16)
        gd_ref[...] += dot_nt(jnp.concatenate([activated, ones], axis=0), branch_low)
        slope = 0.5 * (1.0 + bend) + (0.5 * GELU_A) * before * (1.0 - bend * bend) * (
            1.0 + (3.0 * GELU_B) * square
        )
        before_low = (dot(wdown_ref[level], branch_low) * slope).astype(BF16)
        gu_ref[...] += dot_nt(jnp.concatenate([first_low, ones], axis=0), before_low)
        first_grad = second + dot(wup_ref[level], before_low)
        gg_ref[2] += first_grad * normed_one
        gg_ref[3] += first_grad
        residual = norm_backward(first_grad, normed_one, inverse_one, gain_one)
        dh_ref[c] = residual
        attended_low = residual.astype(BF16)
        go_ref[...] += dot_nt(jnp.concatenate([mixed_low, ones], axis=0), attended_low)
        mixed_grad = dot(wout_ref[level], attended_low).astype(BF16)
        product = mixed_grad.astype(F32) * mixed
        for t in range(2):
            sl = slice(t * BLK, (t + 1) * BLK)
            b = 2 * c + t
            pull = head_stack(mixed_grad[:, sl])
            dots = [
                jnp.sum(product[h * head : (h + 1) * head, sl], axis=0, keepdims=True)
                for h in range(HEADS)
            ]
            if single:
                prob = dot(v_ref[b], pull)
                lows, grads, parts = [], [], []
                for h in range(HEADS):
                    hs = slice(h * BLK, (h + 1) * BLK)
                    a = a_ref[t, :, hs]
                    g = (a * (prob[:, hs] - dots[h])).astype(BF16)
                    lows.append(a.astype(BF16))
                    grads.append(g)
                    parts.append(dot(kt_ref[b, h * head : (h + 1) * head, :], g))
                dv_ref[b] = dot_nt(jnp.concatenate(lows, axis=1), pull)
                dk_ref[b] = dot_nt(jnp.concatenate(grads, axis=1), stacks[t])
                dq = jnp.concatenate(parts, axis=0)
            else:
                masked_of, lo, hi = stats[t]
                stat_ref[t, 2] = whole_rows(jnp.concatenate(dots, axis=1))
                stack_ref[t, 1] = pull

                def step_back(j, dq, t=t, masked_of=masked_of):
                    stack, pull = stack_ref[t, 0], stack_ref[t, 1]
                    top, inv, dots_row = stat_ref[t, 0], stat_ref[t, 1], stat_ref[t, 2]
                    a = jnp.exp(tiles(masked_of(j)) - top[None]) * inv[None]
                    g = a * (tiles(dot(v_ref[j], pull)) - dots_row[None])
                    a = a.reshape(BLK, HEADS * BLK)
                    g = g.reshape(BLK, HEADS * BLK).astype(BF16)
                    dv_ref[j] += dot_nt(a.astype(BF16), pull)
                    dk_ref[j] += dot_nt(g, stack)
                    return dq + own_heads(dot(kt_ref[j], g))

                dq = lax.fori_loop(lo, hi, step_back, jnp.zeros((width, BLK), F32))
            dq_ref[c, :, sl] = (dq * scale).astype(BF16)

    @pl.loop(0, chunks)
    def _(c):
        @pl.when(jnp.logical_not(several))
        def _():
            chunk(c, True)

        @pl.when(several)
        def _():
            chunk(c, False)

    if mode == "fwd":
        for r in range(acc_ref.shape[0] // BLK):
            sl = slice(r * BLK, (r + 1) * BLK)
            msg_ref[sl, :] = acc_ref[sl, :].astype(BF16)
        return

    @pl.loop(0, chunks)
    def _(c):
        dq = dq_ref[c]
        dk = jnp.concatenate([dk_ref[2 * c], dk_ref[2 * c + 1]], axis=0).astype(BF16)
        dv = jnp.concatenate([dv_ref[2 * c], dv_ref[2 * c + 1]], axis=0).astype(BF16)
        dx = (
            dh_ref[c]
            + dot(wqkv_ref[level, :, :width], dq)
            + dot_nt(wqkv_ref[level, :, width : 2 * width], dk)
            + dot_nt(wqkv_ref[level, :, 2 * width :], dv)
        )
        joined = ut_ref[c]
        gq_ref[0] += dot_nt(joined, dq)
        gq_ref[1] += dot(joined, dk)
        gq_ref[2] += dot(xt_ref[c], dv)
        high = dx.astype(BF16)
        if mode == "mid":
            pair = jnp.concatenate([yt_ref[c], high], axis=0)
        else:
            pair = jnp.concatenate([high, (dx - high.astype(F32)).astype(BF16)], axis=0)
        for r in range(total // 256):
            sl = slice(r * 256, (r + 1) * 256)
            acc_ref[sl, :] += dot_nt(pick_ref[c, sl, :], pair)

    for r in range(total // BLK):
        sl = slice(r * BLK, (r + 1) * BLK)
        if mode == "mid":
            back_ref[sl, :] = acc_ref[sl, :].astype(BF16)
        else:
            back_ref[sl, :] = acc_ref[sl, :width] + acc_ref[sl, width:]
    wg = functools.partial(jnp.concatenate, axis=0)
    for b in range(3):
        wg_ref[b * BLK : (b + 1) * BLK, :] = gq_ref[b].astype(BF16)
    wg_ref[384:512, :] = go_ref[:width].astype(BF16)
    for b in range(2):
        sl = slice(b * BLK, (b + 1) * BLK)
        wg_ref[512 + b * BLK : 640 + b * BLK, :] = gu_ref[:width, sl].astype(BF16)
    wg_ref[768:1024, :] = gd_ref[:256].astype(BF16)
    sums = []
    for i in range(4):
        both = gg_ref[i, :, :BLK] + gg_ref[i, :, BLK:]
        sums.append(jnp.sum(jnp.transpose(both), axis=0, keepdims=True))
    out_bias, down_bias = go_ref[width : width + 1], gd_ref[256:257]
    up_bias = gu_ref[width : width + 1]
    small = [
        sums[2], sums[0], out_bias, sums[3], down_bias, sums[1], up_bias[:, :BLK], up_bias[:, BLK:],
        jnp.zeros((8, BLK), F32),
    ]
    wg_ref[1024:GRAD_ROWS, :] = wg(small).astype(BF16)


def run_layer(mode, level, cap, buffer_rows, *args):
    total = args[0].shape[1]
    width = 128
    nb = total // 64
    nc = nb // 2
    extra = 3 if mode == "mid" else 2
    vm = pltpu.VMEM
    if mode == "fwd":
        out_shape = jax.ShapeDtypeStruct((buffer_rows, width), BF16)
        acc = vm((buffer_rows, width), F32)
    else:
        acc = vm((total, 2 * width), F32)
        out_shape = (
            jax.ShapeDtypeStruct((total, 2 * width), BF16)
            if mode == "mid"
            else jax.ShapeDtypeStruct((total, width), F32),
            jax.ShapeDtypeStruct((GRAD_ROWS, width), BF16),
        )
    chunked = lambda dt: vm((nc, width, CH), dt)
    blocked = lambda dt: vm((nb, BLK, BLK), dt)
    scratch = [
        vm((WINDOWS, BLK), I32), vm((WINDOWS, BLK), I32), vm((total, BLK), I32),
        vm((extra * width + 16, total), BF16), vm((nc, total, CH), BF16), acc,
        vm((384, width), BF16), vm((width, width), BF16), vm((256, width), BF16), vm((width, 256), BF16),
        vm((8, BLK, BLK), F32),
        chunked(BF16), chunked(BF16), chunked(BF16),
        blocked(BF16), blocked(BF16), blocked(BF16), blocked(BF16),
        vm((nc, 8, CH), F32), blocked(F32), vm((nc, 8, CH), I32),
    ]
    if mode != "fwd":
        scratch += [
            chunked(BF16), chunked(BF16), chunked(F32), chunked(BF16), blocked(F32), blocked(F32),
            vm((2, BLK, HEADS * BLK), F32),
            vm((3, width, width), F32), vm((width + 16, width), F32), vm((width + 16, 256), F32),
            vm((256 + 16, width), F32), vm((4, width, CH), F32),
        ]
        if mode == "bwd":
            scratch += [vm((width, buffer_rows), BF16)]
    scratch += [vm((2, 3, 8, HEADS * BLK), F32), vm((2, 2, width, HEADS * BLK), BF16), pltpu.SMEM((2, nb), I32)]
    spec = pl.BlockSpec(memory_space=pltpu.VMEM)
    return pl.pallas_call(
        functools.partial(layer_kernel, mode, level, cap),
        out_shape=out_shape,
        in_specs=[spec] * len(args),
        out_specs=spec if mode == "fwd" else (spec, spec),
        scratch_shapes=scratch,
        compiler_params=pltpu.CompilerParams(vmem_limit_bytes=VMEM),
        name="layer_" + mode,
    )(*args)


def send_kernel(cap, meta_ref, pos_ref, cot_ref, out_ref):
    strips = out_ref.shape[0]
    total = meta_ref.shape[1]
    meta = meta_ref[...]
    place = jnp.where(meta[3:4] > 0, meta[0:1] * cap + meta[1:2], -1)
    source = jnp.concatenate([pos_ref[1], cot_ref[...]], axis=1)
    at = iota((16, total), 0)
    rows = jnp.where(at == 0, meta[2:3], jnp.where(at == 1, meta[3:4], 0)).astype(F32).astype(BF16)
    spot = iota((cap, total), 0)
    for d in range(strips):
        hot = (spot + d * cap == place).astype(F32).astype(BF16)
        out_ref[d, :cap, :] = dot(hot, source).astype(BF16)
        out_ref[d, cap:, :] = jnp.zeros((16, 256), BF16)
        out_ref[d, cap:, :cap] = dot_nt(rows, hot).astype(BF16)


def fetch_kernel(place_ref, rows_ref, out_ref):
    total = out_ref.shape[0]
    buffer_rows = rows_ref.shape[0]
    at = iota((BLK, buffer_rows), 1)
    for b in range(total // BLK):
        sl = slice(b * BLK, (b + 1) * BLK)
        col = column(place_ref[:, sl].astype(F32)).astype(I32)
        wide = jnp.concatenate([col] * (buffer_rows // BLK), axis=1)
        hot = (wide == at).astype(F32).astype(BF16)
        out_ref[sl, :] = dot(hot, rows_ref[...]).astype(BF16)


def local(
    features, position, cotangent, w_qkv, w_out, w_up, w_down, b_up, gains, shifts,
    window, shifted_window, dest, slot, valid,
):
    strips = lax.axis_size("strip")
    devices = strips * lax.axis_size("sub")
    rows, width = features.shape
    cap = 2 * rows // strips
    buffer_rows = strips * cap
    weights = (w_qkv, w_out, w_up, w_down, b_up, gains, shifts)
    spec = pl.BlockSpec(memory_space=pltpu.VMEM)
    params = pltpu.CompilerParams(vmem_limit_bytes=VMEM)

    send = pl.pallas_call(
        functools.partial(send_kernel, cap),
        out_shape=jax.ShapeDtypeStruct((strips, cap + 16, 2 * width), BF16),
        in_specs=[spec] * 3,
        out_specs=spec,
        compiler_params=params,
        name="send",
    )(jnp.stack([dest, slot, shifted_window, valid]), position, cotangent)
    arrived = lax.all_to_all(send, "strip", split_axis=0, concat_axis=0, tiled=True)

    meta_zero = jnp.stack([window, valid, dest, slot])
    message = run_layer("fwd", 0, cap, buffer_rows, meta_zero, features, position, *weights)
    moved = lax.all_to_all(message, "strip", split_axis=0, concat_axis=0, tiled=True)

    meta_one = arrived[:, cap : cap + 2, :cap].transpose(1, 0, 2).reshape(2, buffer_rows).astype(F32)
    rest = arrived[:, :cap].reshape(buffer_rows, 2 * width)
    back, grads_one = run_layer("mid", 1, cap, buffer_rows, meta_one, rest, moved, *weights)
    returned = lax.all_to_all(back, "strip", split_axis=0, concat_axis=0, tiled=True)

    grad_features, grads_zero = run_layer(
        "bwd", 0, cap, buffer_rows, meta_zero, features, position, returned[:, width:], *weights
    )
    place = jnp.where(valid > 0, dest * cap + slot, -1)[None]
    output = pl.pallas_call(
        fetch_kernel,
        out_shape=jax.ShapeDtypeStruct((rows, width), BF16),
        in_specs=[spec] * 2,
        out_specs=spec,
        compiler_params=params,
        name="fetch",
    )(place, returned[:, :width])

    both = jnp.concatenate([grads_zero, grads_one], axis=0)
    share = -(-both.shape[0] // (8 * devices)) * 8
    both = jnp.pad(both, ((0, share * devices - both.shape[0]), (0, 0)))
    axes = ("strip", "sub")
    parts = lax.all_to_all(both, axes, split_axis=0, concat_axis=0, tiled=True)
    mine = jnp.sum(parts.reshape(devices, share, width).astype(F32), axis=0).astype(BF16)
    whole = lax.all_to_all(
        jnp.tile(mine, (devices, 1)), axes, split_axis=0, concat_axis=0, tiled=True
    ).astype(F32)
    sums = whole[: 2 * GRAD_ROWS].reshape(2, GRAD_ROWS, width)
    wide = lambda lo, n: jnp.concatenate(
        [sums[:, lo + i * BLK : lo + (i + 1) * BLK] for i in range(n)], axis=2
    )
    return (
        output,
        grad_features,
        wide(0, 3),
        sums[:, 384:512],
        wide(512, 2),
        sums[:, 768:1024],
        sums[:, 1030:1032].reshape(2, 256),
        sums[:, 1024:1026],
        sums[:, 1026:1030],
    )


def solution(mesh):
    rows = P(("strip", "sub"), None)
    flat = P(("strip", "sub"))
    placed = (rows, P(None, ("strip", "sub"), None), rows) + (P(),) * 7 + (flat,) * 5
    return jax.shard_map(
        local,
        mesh=mesh,
        in_specs=placed,
        out_specs=(rows, rows) + (P(),) * 7,
        check_vma=False,
    )
```

time: 1020 us -> 212 us (0.21); the launches traced: 1010 us -> 214 us
  matrix products: 478 us -> 0 us
  other arithmetic: 243 us -> 5.31 us
  waiting for transfers between devices: 121 us -> 37.2 us
  local copies, waits for them, and re-layouts: 83.3 us -> 7.03 us
  Pallas kernels: 0 us -> 72.6 us
  blocking collectives: 41.1 us -> 76.8 us
  between operations: 16 us -> 0.7 us
  starting transfers between devices: 24.8 us -> 14.2 us
    dot_general x72 -> x0, matrix products: 478 us -> none  [the longest x12 178 us: block_scores(): jnp.einsum('ihd,jhd->hij', query_blk, head_keys, preferred_element_type=j...]
    convert_element_type x12 -> x1, other arithmetic: 134 us -> 0.61 us  [local(): arrived[:, cap:cap + 2, :cap].transpose(1, 0, 2).reshape(2, buffer_rows)]
    psum x1 -> x0, waiting for transfers between devices: 91.1 us -> none  [local(): totals = lax.psum(stacked, ('strip', 'sub'))]
    reduce_sum x17 -> x1, other arithmetic: 83.7 us -> 0.1 us  [local(): jnp.sum(parts.reshape(devices, share, width).astype(F32), axis=0)]
    all_to_all x0 -> x2, blocking collectives: none -> 76.8 us  [the longest x1 50 us: local(): lax.all_to_all(back, 'strip', split_axis=0, concat_axis=0, tiled=True)]
    pallas_call x0 -> x5, Pallas kernels: none -> 72.6 us  [the longest x3 65.1 us: run_layer(): pl.pallas_call(functools.partial(layer_kernel, mode, level, cap), out_sha...]
    psum x1 -> x0, blocking collectives: 41.1 us -> none  [local(): totals = lax.psum(stacked, ('strip', 'sub'))]
    scatter x3 -> x0, local copies, waits for them, and re-layouts: 13.8 us -> none  [spread(): jnp.zeros((buffer_rows, source.shape[1]), source.dtype).at[place]]
  transfers between devices with their start and end apart: 6 -> 3, of which waited for: 4 -> 3; matrix products, arithmetic and copies ran while one was open for 17% -> 1% of each run, Pallas kernels for 0% -> 9%
where the time goes in v1:
time: 212 us; the launch traced here: 214 us
  blocking collectives  76.8 us (36%)
  Pallas kernels  72.6 us (34%)
  waiting for transfers between devices  37.2 us (18%)
  starting transfers between devices  14.2 us (7%)
  local copies, waits for them, and re-layouts  7.03 us (3%)
  other arithmetic  5.31 us (3%)
    pallas_call x3, Pallas kernels, run_layer(): pl.pallas_call(functools.partial(layer_kernel, mode, level, cap), out_sha...  65.1 us
    all_to_all x1, blocking collectives, local(): lax.all_to_all(back, 'strip', split_axis=0, concat_axis=0, tiled=True)  50 us
    all_to_all x1, blocking collectives, local(): parts = lax.all_to_all(both, axes, split_axis=0, concat_axis=0, tiled=True)  26.8 us
    all_to_all x1, waiting for transfers between devices, local(): lax.all_to_all(message, 'strip', split_axis=0, concat_axis=0, tiled=True)  13 us
    all_to_all x1, waiting for transfers between devices, local(): lax.all_to_all(jnp.tile(mine, (devices, 1)), axes, split_axis=0, concat_a...  13 us
    all_to_all x1, waiting for transfers between devices, local(): lax.all_to_all(send, 'strip', split_axis=0, concat_axis=0, tiled=True)  11.2 us
    all_to_all x1, starting transfers between devices, local(): lax.all_to_all(send, 'strip', split_axis=0, concat_axis=0, tiled=True)  7.25 us
    pallas_call x1, Pallas kernels, local(): pl.pallas_call(functools.partial(send_kernel, cap), out_shape=jax.ShapeDt...  4.44 us
  transfers between devices with their start and end apart: 3, of which 3 were waited for; matrix products, arithmetic and copies ran while one was open for 1% of the time, Pallas kernels for 9%

profile of v1, /device:TPU:0, one launch (start us, length us, event | category | flops | bytes accessed | tf_op | source)
XLA Modules:
  0.0 213.9 jit_solution(1822631259053019373)
XLA Ops:
  0.6 1.4 pad_add_fusion.1
  2.1 4.4 %send.1 = bf16[8,272,256]{2,1,0:T(8,128)(2,1)} custom-call(s32[4,1024]{1,0:T(4,128)} %get-tuple-element.26.meta_ref, bf16[2,1024,128]{2,1,0:T(8,128)(2,1)} %refs_2_.3, bf16[1024,128]{1,0:T(8,128)(2,1)} %cot_ref.1), custom_call_target="tpu_custom_call" | custom-call | tf_op jit(solution)/shard_map/send/pallas_call | solution.py:581
  6.5 7.3 %all-to-all-start = ((bf16[8,272,256]{2,1,0:T(8,128)(2,1)}), bf16[8,272,256]{2,1,0:T(8,128)(2,1)S(1)}, u32[]{:S(2)}, u32[]{:S(2)}) async-start(bf16[8,272,256]{2,1,0:T(8,128)(2,1)} %send.1), calls=%async_computation | async-start | bytes 2228224 | tf_op jit(solution)/shard_map/all_to_all | solution.py:589
  13.8 15.9 %layer_fwd.1 = bf16[2048,128]{1,0:T(8,128)(2,1)} custom-call(s32[4,1024]{1,0:T(4,128)} %get-tuple-element.25.refs_0_, bf16[1024,128]{1,0:T(8,128)(2,1)} %refs_1_.3, bf16[2,1024,128]{2,1,0:T(8,128)(2,1)} %refs_2_.3, bf16[2,128,384]{2,1,0:T(8,128)(2,1)} %refs_4_.5, bf16[2,128,128]{2,1,0:T(8,128)(2,1)} %refs_5_.5, bf16[2,128,256]{2,1,0:T(8,128)(2,1)} %refs_6_.5, ...), custom_call_target="tpu_custom_call" | custom-call | tf_op jit(solution)/shard_map/layer_fwd/pallas_call | solution.py:529
  29.7 11.2 %all-to-all-done = bf16[8,272,256]{2,1,0:T(8,128)(2,1)S(1)} async-done(((bf16[8,272,256]{2,1,0:T(8,128)(2,1)}), bf16[8,272,256]{2,1,0:T(8,128)(2,1)S(1)}, u32[]{:S(2)}, u32[]{:S(2)}) %all-to-all-start) | async-done | bytes 1114144 | tf_op jit(solution)/shard_map/all_to_all | solution.py:589
  41.0 3.6 %all-to-all-start.1 = ((bf16[8,256,128]{2,1,0:T(8,128)(2,1)}), bf16[8,256,128]{2,1,0:T(8,128)(2,1)S(1)}, u32[]{:S(2)}, u32[]{:S(2)}) async-start(bf16[8,256,128]{2,1,0:T(8,128)(2,1)} %bitcast.32), calls=%async_computation.1 | async-start | bytes 1048576 | tf_op jit(solution)/shard_map/all_to_all | solution.py:593
  44.6 1.0 slice.62
  45.6 0.6 slice_convert_fusion
  46.2 13.0 %all-to-all-done.1 = bf16[8,256,128]{2,1,0:T(8,128)(2,1)S(1)} async-done(((bf16[8,256,128]{2,1,0:T(8,128)(2,1)}), bf16[8,256,128]{2,1,0:T(8,128)(2,1)S(1)}, u32[]{:S(2)}, u32[]{:S(2)}) %all-to-all-start.1) | async-done | bytes 524320 | tf_op jit(solution)/shard_map/all_to_all | solution.py:593
  59.3 0.0 copy-start
  59.3 0.8 copy-done
  60.1 22.8 %layer_mid.1 = (bf16[2048,256]{1,0:T(8,128)(2,1)}, bf16[1040,128]{1,0:T(8,128)(2,1)}) custom-call(f32[2,2048]{1,0:T(2,128)} %bitcast.35, bf16[2048,256]{1,0:T(8,128)(2,1)} %bitcast.28, bf16[2048,128]{1,0:T(8,128)(2,1)} %bitcast.33, bf16[2,128,384]{2,1,0:T(8,128)(2,1)} %refs_4_.5, bf16[2,128,128]{2,1,0:T(8,128)(2,1)} %refs_5_.5, ...), custom_call_target="tpu_custom_call" | custom-call | tf_op jit(solution)/shard_map/layer_mid/pallas_call | solution.py:529
  82.9 50.0 %all_to_all.43 = bf16[8,256,256]{2,1,0:T(8,128)(2,1)S(1)} all-to-all(bf16[8,256,256]{2,1,0:T(8,128)(2,1)} %bitcast.34), channel_id=1, replica_groups=mesh['strip'=8,'sub'=4] {'strip'}, dimensions={0} | all-to-all | bytes 2097152 | tf_op jit(solution)/shard_map/all_to_all | solution.py:598
  132.9 1.1 fusion.3
  133.9 0.0 copy-start.1
  133.9 26.4 %layer_bwd.1 = (f32[1024,128]{1,0:T(8,128)}, bf16[1040,128]{1,0:T(8,128)(2,1)}) custom-call(s32[4,1024]{1,0:T(4,128)} %get-tuple-element.25.refs_0_, bf16[1024,128]{1,0:T(8,128)(2,1)} %refs_1_.3, bf16[2,1024,128]{2,1,0:T(8,128)(2,1)} %refs_2_.3, bf16[2048,128]{1,0:T(8,128)(2,1)} %get-tuple-element.17.refs_3_, bf16[2,128,384]{2,1,0:T(8,128)(2,1)} %refs_4_.5, ...), custom_call_target="tpu_custom_call" | custom-call | tf_op jit(solution)/shard_map/layer_bwd/pallas_call | solution.py:529
  160.3 0.0 copy-done.1
  160.3 1.0 fusion.2
  161.3 26.8 %all_to_all.44 = bf16[32,72,128]{2,1,0:T(8,128)(2,1)S(1)} all-to-all(bf16[32,72,128]{2,1,0:T(8,128)(2,1)S(1)} %bitcast.30), channel_id=1, replica_groups=mesh['strip'=8,'sub'=4] {'strip','sub'}, dimensions={0} | all-to-all | bytes 1179648 | tf_op jit(solution)/shard_map/all_to_all | solution.py:617
  188.1 0.0 copy-start.2
  188.1 0.0 copy-start.3
  188.1 0.0 copy-start.4
  188.1 0.1 reduce_sum.12
  188.2 0.9 tile.2
  189.1 3.3 %all-to-all-start.4 = ((bf16[32,72,128]{2,1,0:T(8,128)(2,1)}), bf16[32,72,128]{2,1,0:T(8,128)(2,1)S(1)}, u32[]{:S(2)}, u32[]{:S(2)}) async-start(bf16[32,72,128]{2,1,0:T(8,128)(2,1)} %tile.2), calls=%async_computation.4 | async-start | bytes 1179648 | tf_op jit(solution)/shard_map/all_to_all | solution.py:619
  192.4 0.0 copy-done.2
  192.4 0.0 copy-done.3
  192.4 0.0 copy-done.4
  192.4 0.6 add_select_fusion
  193.0 3.1 %fetch.1 = bf16[1024,128]{1,0:T(8,128)(2,1)} custom-call(s32[1,1024]{1,0:T(1,128)} %bitcast.36, bf16[2048,128]{1,0:T(8,128)(2,1)} %get-tuple-element.18.rows_ref), custom_call_target="tpu_custom_call" | custom-call | tf_op jit(solution)/shard_map/fetch/pallas_call | solution.py:604
  196.1 13.0 %all-to-all-done.4 = bf16[32,72,128]{2,1,0:T(8,128)(2,1)S(1)} async-done(((bf16[32,72,128]{2,1,0:T(8,128)(2,1)}), bf16[32,72,128]{2,1,0:T(8,128)(2,1)S(1)}, u32[]{:S(2)}, u32[]{:S(2)}) %all-to-all-start.4) | async-done | bytes 589856 | tf_op jit(solution)/shard_map/all_to_all | solution.py:619
  209.1 0.7 fusion.4
  209.9 0.7 slice.72
  210.6 0.1 convert.6
  210.7 0.6 slice.74
  211.2 0.6 slice.75
  211.8 0.6 copy.26
  212.4 0.7 pad_maximum_fusion.1
  213.1 0.8 pad_maximum_fusion
  (2 shorter events, 0.0 us)
Async XLA Ops:
  6.5 34.4 %all-to-all-start = ((bf16[8,272,256]{2,1,0:T(8,128)(2,1)}), bf16[8,272,256]{2,1,0:T(8,128)(2,1)S(1)}, u32[]{:S(2)}, u32[]{:S(2)}) async-start(bf16[8,272,256]{2,1,0:T(8,128)(2,1)} %send.1), calls=%async_computation | async-start | bytes 2228224 | tf_op jit(solution)/shard_map/all_to_all | solution.py:589
  41.0 18.3 %all-to-all-start.1 = ((bf16[8,256,128]{2,1,0:T(8,128)(2,1)}), bf16[8,256,128]{2,1,0:T(8,128)(2,1)S(1)}, u32[]{:S(2)}, u32[]{:S(2)}) async-start(bf16[8,256,128]{2,1,0:T(8,128)(2,1)} %bitcast.32), calls=%async_computation.1 | async-start | bytes 1048576 | tf_op jit(solution)/shard_map/all_to_all | solution.py:593
  59.3 0.8 copy-start
  133.9 26.4 %copy-start.1 = (bf16[1040,128]{1,0:T(8,128)(2,1)S(1)}, bf16[1040,128]{1,0:T(8,128)(2,1)}, u32[]{:S(2)}) copy-start(bf16[1040,128]{1,0:T(8,128)(2,1)} %get-tuple-element.16) | copy-start | bytes 798724
  188.1 4.3 %copy-start.2 = (s32[1024]{0:T(1024)S(1)}, s32[1024]{0:T(1024)}, u32[]{:S(2)}) copy-start(s32[1024]{0:T(1024)} %param.28) | copy-start | bytes 12292
  188.1 4.3 %copy-start.3 = (s32[1024]{0:T(1024)S(1)}, s32[1024]{0:T(1024)}, u32[]{:S(2)}) copy-start(s32[1024]{0:T(1024)} %param.27) | copy-start | bytes 12292
  188.1 4.3 %copy-start.4 = (s32[1024]{0:T(1024)S(1)}, s32[1024]{0:T(1024)}, u32[]{:S(2)}) copy-start(s32[1024]{0:T(1024)} %param.29) | copy-start | bytes 12292
  189.1 20.0 %all-to-all-start.4 = ((bf16[32,72,128]{2,1,0:T(8,128)(2,1)}), bf16[32,72,128]{2,1,0:T(8,128)(2,1)S(1)}, u32[]{:S(2)}, u32[]{:S(2)}) async-start(bf16[32,72,128]{2,1,0:T(8,128)(2,1)} %tile.2), calls=%async_computation.4 | async-start | bytes 1179648 | tf_op jit(solution)/shard_map/all_to_all | solution.py:619
